TPU v7x, 128 devices: a whole 4x4x4 slice. The times are simulated.
128 devices in a mesh: frame: 16 (over y, x), height: 8 (over z, core).
Axes of the slice: x: 4, y: 4, z: 4, core: 2. Of those that a mesh axis runs over, the one named last changes fastest.
Arguments:
- tokens: bfloat16 [16, 106496], P(None, ('frame', 'height')), may hold values from -8 to 8
- token_pos: int32 [106496], P('frame'), may hold values from 0 to 106495, as said below
- weight_in: bfloat16 [3, 3, 3, 16, 512], replicated, may hold values from -0.3125 to 0.3125
- bias_in: float32 [512], replicated, may hold values from -1.8 to 1.8
- gain_one: float32 [512], replicated, may hold values from 0.1 to 1.9
- offset_one: float32 [512], replicated, may hold values from -3 to 3
- weight_one: bfloat16 [3, 3, 3, 512, 512], P(None, None, None, None, 'height'), may hold values from -0.0546875 to 0.0546875
- bias_one: float32 [512], replicated, may hold values from -1.8 to 1.8
- gain_two: float32 [512], replicated, may hold values from 0.1 to 1.9
- offset_two: float32 [512], replicated, may hold values from -3 to 3
- weight_two: bfloat16 [3, 3, 3, 512, 512], P(None, None, None, None, 'height'), may hold values from -0.0546875 to 0.0546875
- bias_two: float32 [512], replicated, may hold values from -1.8 to 1.8
- weight_time: bfloat16 [3, 512, 1024], replicated, may hold values from -0.15625 to 0.15625
- bias_time: float32 [1024], replicated, may hold values from -1.8 to 1.8
Outputs:
- frames_out: bfloat16 [64, 64, 208, 512], P('frame', 'height')
Inputs may be any that keep to these rules, and one draw needn't show every extreme that they name: token_pos is a permutation of 0 .. 106495. The 832 entries of shard s = f * 8 + b (the shard's part of tokens along the frame+height split) are positions of frame slab f only (frames f * 2 .. f * 2 + 1), and hold exactly 104 positions of each height tile (rows g * 4 .. g * 4 + 3).
All inputs are finite; a program needn't handle non-finite values.
Results may differ from a plain program's by a relative error of at most 0.008.
Values may be sent and summed in bfloat16 or wider, within the bound.
No kernel may reach another device: no remote copies, remote signals or barrier semaphores. Data moves between devices by JAX's collectives and lax.ppermute only.
A program may use at most 192 MiB of HBM per device.

v0:
```python
import functools

import jax
import jax.numpy as jnp
from jax import lax
from jax.experimental import pallas as pl
from jax.experimental.pallas import tpu as pltpu
from jax.sharding import PartitionSpec as P

GROUPS = 32
ZC = 16
FT = 2
RH = 4
WD = 104
WP = 112
CH = 512
CELLS = FT * RH * WD
F32 = jnp.float32
BF16 = jnp.bfloat16
NT = (((1,), (1,)), ((), ()))
TN = (((0,), (0,)), ((), ()))
VMEM = pl.BlockSpec(memory_space=pltpu.VMEM)
SMEM = pl.BlockSpec(memory_space=pltpu.SMEM)
ANY = pl.BlockSpec(memory_space=pl.ANY)
EXACT = lax.Precision.HIGHEST
LIMIT = 56 * 2**20


def along(value, axis, steps):
    count = lax.axis_size(axis)
    leading, last = (max(0, -steps), min(count, count - steps))
    return lax.ppermute(value, axis, [(source, source + steps) for source in range(leading, last)])


def spread(rows, cols, lanes_first, shift):
    one = lax.broadcasted_iota(jnp.int32, (rows, cols), 0)
    two = lax.broadcasted_iota(jnp.int32, (rows, cols), 1)
    lane, channel = (one, two) if lanes_first else (two, one)
    return (lane == channel // (CH // GROUPS) + shift).astype(F32)


def local_stats(values, stat_ref):
    cells = values.shape[0]
    total = jnp.broadcast_to(jnp.sum(values, axis=0, keepdims=True), (8, CH))
    size = cells * (CH // GROUPS)
    mean = jnp.dot(total, spread(CH, 128, False, 0), precision=EXACT, preferred_element_type=F32) / size
    per_channel = jnp.dot(mean, spread(128, CH, True, 0), precision=EXACT, preferred_element_type=F32)
    centered = values - per_channel[:1]
    square = jnp.broadcast_to(jnp.sum(centered * centered, axis=0, keepdims=True), (8, CH))
    spread_sq = jnp.dot(square, spread(CH, 128, False, GROUPS), precision=EXACT, preferred_element_type=F32)
    stat_ref[...] = jnp.broadcast_to((mean + spread_sq)[:1], stat_ref.shape)


def combine_stats(stats_ref, size):
    stats = stats_ref[...]
    devices = stats.shape[0]
    means = jnp.dot(stats, spread(128, CH, True, 0), precision=EXACT, preferred_element_type=F32)
    squares = jnp.dot(stats, spread(128, CH, True, GROUPS), precision=EXACT, preferred_element_type=F32)
    mean = jnp.sum(means, axis=0, keepdims=True) / devices
    away = means - mean
    total = jnp.sum(squares + size * (away * away), axis=0, keepdims=True)
    return mean, lax.rsqrt(total / (size * devices) + 1e-06)


def share_stats(stat):
    return lax.all_to_all(stat, ("frame", "height"), 0, 0, tiled=True)


def input_kernel(early_ref, behind_ref, own_ref, w_ref, bias_ref, base_ref, stat_ref):
    w = w_ref[...]
    lat = {}
    for k, ref in enumerate((early_ref, behind_ref, own_ref)):
        for i in range(FT):
            for r in range(RH + 4):
                value = ref[i, r].astype(F32)
                shifts = [value] + [pltpu.roll(value, 128 - e, 1) for e in (1, 2)]
                lat[k * FT + i, r] = jnp.concatenate([v.astype(BF16) for v in shifts], axis=0)
    for t in range(2 * FT):
        columns = []
        for r in range(RH + 2):
            columns.append(jnp.concatenate([lat[t + a, r + b] for a in range(3) for b in range(3)], axis=0))
        field = jnp.concatenate(columns, axis=1)
        total = lax.dot_general(field, w, TN, preferred_element_type=F32)
        total = (total + bias_ref[...]).astype(BF16).reshape(RH + 2, 128, CH)
        base_ref[t] = total[:, :WD]
    own = base_ref[FT:, 1 : RH + 1].reshape(CELLS, CH).astype(F32)
    local_stats(own, stat_ref)


def input_conv(latent, weight, bias, devices):
    return pl.pallas_call(
        input_kernel,
        in_specs=[VMEM] * 5,
        out_specs=[VMEM, VMEM],
        out_shape=[
            jax.ShapeDtypeStruct((2 * FT, RH + 2, WD, CH), BF16),
            jax.ShapeDtypeStruct((devices, 128), F32),
        ],
        compiler_params=pltpu.CompilerParams(vmem_limit_bytes=LIMIT),
        cost_estimate=pl.CostEstimate(flops=3 * 10**9, bytes_accessed=4 * 10**6, transcendentals=0),
        name="input_conv",
    )(*latent, weight, bias)


def ring_gather(unit, send, pos):
    units = unit.shape[0]
    quarter = lax.dynamic_slice_in_dim(unit, pos * 16, 16, axis=2)
    tiles = lax.axis_size("height")
    over = lambda k: [(i, (i + 2 * k) % tiles) for i in range(tiles)]
    piece = jnp.concatenate([lax.ppermute(quarter, "height", over(k)) for k in (1, 3, 2)], axis=0)
    half = (piece.shape[0] + 1) // 2
    left, right = send(piece, 1), send(piece, -1)
    left2, right2 = send(left[:half], 1), send(right[half:], -1)
    quarters = [unit[:, :, 16 * k : 16 * k + 16] for k in range(4)]
    held = jnp.concatenate([piece, left, right, left2, right2, *quarters], axis=0)
    other = lax.ppermute(held, "height", [(i, i ^ 1) for i in range(tiles)])
    return [piece, left, right, left2, right2, unit, other], units, half


def ring_plan(arrays, units, half, columns, axis, first):
    plan = []
    full = 3 * units

    def add(array, start, low, high, flip, place):
        index = low
        while index < high:
            stop = min(high, index - index % 3 + 3)
            shift, e, a = index // units, index % units // 3, index % 3
            z = 0 if place == "own" else (3, 1, 2)[shift]
            plan.append((array, start + index - low, stop - index, columns[e], a, 16, (flip, z, axis, place)))
            index = stop

    for flip in (0, 1):
        base = 0
        for k, (low, high, ring) in enumerate([(0, full, 0), (0, full, 3), (0, full, 1), (0, half, 2), (half, full, 2)]):
            add(first + (6 if flip else k), base if flip else 0, low, high, flip, ring)
            base += high - low
        for q in range(4 if flip else 1):
            for u in range(units // 3):
                start = (base + q * units if flip else 0) + 3 * u
                rows = 16 if flip else 64
                plan.append((first + (6 if flip else 5), start, 3, columns[u], 0, rows, (flip, 0, None, q)))
    return arrays, plan


def conv_kernel(pieces, products, taps, plan, weights, extras, *refs):
    refs = list(refs)
    raws = [refs.pop(0) for _ in pieces]
    stats_ref, flags_ref, place_ref, gain_ref, offset_ref = [refs.pop(0) for _ in range(5)]
    w_refs = [refs.pop(0) for _ in range(weights)]
    partial_ref = refs.pop(0) if "partial" in extras else None
    bias_ref = refs.pop(0) if "bias" in extras else None
    base_ref = refs.pop(0) if "base" in extras else None
    out_ref = refs.pop(0)
    stat_ref = refs.pop(0) if "stat" in extras else None
    field, wbuf, acc, sems = refs
    low, high = taps[0], taps[-1] + 1
    z, core = place_ref[0], place_ref[1]
    for e in range(3):
        for array, start, length, column, a, rows, where in plan:
            if column != e:
                continue
            begin, end = max(a, low), min(a + length, high)
            if begin >= end:
                continue
            if where is None:
                source = w_refs[array].at[pl.ds(begin, end - begin), :, start]
                target = wbuf.at[e, pl.ds(begin - low, end - begin)]
            else:
                flip, shift, ring, step = where
                block = lax.rem(z + shift, 4) * 2 + (1 - core if flip else core)
                quarter = step if ring is None else lax.rem(place_ref[ring] + step, 4)
                offset = pl.multiple_of(block * 64 + quarter * 16, 16)
                source = w_refs[array].at[pl.ds(start + begin - a, end - begin)]
                target = wbuf.at[e, pl.ds(begin - low, end - begin), :, pl.ds(offset, rows)]
            pltpu.make_async_copy(source, target, sems.at[e]).start()
    mean, inverse = combine_stats(stats_ref, CELLS * (CH // GROUPS))
    scale = inverse * gain_ref[...]
    offset = offset_ref[...]
    for raw, (frame, frames, row, rows, flag_of) in zip(raws, pieces):
        for i in range(frames):
            for j in range(rows):
                value = (raw[i, j].astype(F32) - mean) * scale + offset
                half = 0.5 * value
                value = half + half * jnp.tanh(half)
                for which in flag_of(i, j):
                    value = value * flags_ref[which]
                field[frame + i, row + j, :WD] = value.astype(BF16)
                field[frame + i, row + j, WD:] = jnp.zeros((WP - WD, CH), BF16)
    for e in range(3):
        pltpu.make_async_copy(wbuf.at[e], wbuf.at[e], sems.at[e]).wait()
        for t in range(FT):
            terms = [(f, a) for (out, f, a) in products if out == t]
            xs = [field[f, b : b + RH].reshape(RH * WP, CH) for f, a in terms for b in range(3)]
            ws = [wbuf[e, a - low, b] for f, a in terms for b in range(3)]
            acc[e, pl.ds(t * RH * WP, RH * WP)] = lax.dot_general(
                jnp.concatenate(xs, axis=1), jnp.concatenate(ws, axis=1), NT, preferred_element_type=F32
            )
    edge = jnp.zeros((1, CH), F32)
    total = acc[1] + jnp.concatenate([edge, acc[0, :-1]], axis=0) + jnp.concatenate([acc[2, 1:], edge], axis=0)
    total = total.reshape(FT, RH, WP, CH)[:, :, :WD]
    if partial_ref is not None:
        total = total + partial_ref[...]
    if bias_ref is not None:
        total = total + bias_ref[...]
    if base_ref is not None:
        total = total + base_ref[FT:, 1 : RH + 1].astype(F32)
    out_ref[...] = total.astype(out_ref.dtype)
    if stat_ref is not None:
        local_stats(total.astype(BF16).astype(F32).reshape(CELLS, CH), stat_ref)


def block_conv(name, raws, pieces, products, stats, flags, place, gain, offset, weight, extras, kind, devices):
    arrays, plan = weight
    taps = sorted({a for _, _, a in products})
    frames = max(f for _, f, _ in products) + 1
    args = [*raws, stats, flags, place, gain, offset, *arrays]
    args += [extras[k] for k in ("partial", "bias", "base") if k in extras]
    specs = [*[VMEM] * len(raws), VMEM, SMEM, SMEM, VMEM, VMEM, *[ANY] * len(arrays)]
    specs += [VMEM] * (len(args) - len(specs))
    shapes = [jax.ShapeDtypeStruct((FT, RH, WD, CH), kind)]
    if "stat" in extras:
        shapes.append(jax.ShapeDtypeStruct((devices, 128), F32))
    return pl.pallas_call(
        functools.partial(conv_kernel, pieces, products, taps, plan, len(arrays), tuple(extras)),
        in_specs=specs,
        out_specs=[VMEM] * len(shapes),
        out_shape=shapes,
        scratch_shapes=[
            pltpu.VMEM((frames, RH + 2, WP, CH), BF16),
            pltpu.VMEM((3, len(taps), 3, CH, CH), BF16),
            pltpu.VMEM((3, FT * RH * WP, CH), F32),
            pltpu.SemaphoreType.DMA((3,)),
        ],
        compiler_params=pltpu.CompilerParams(vmem_limit_bytes=LIMIT),
        cost_estimate=pl.CostEstimate(
            flops=len(products) * 2 * 9 * RH * WP * CH * CH, bytes_accessed=16 * 10**6, transcendentals=0
        ),
        name=name,
    )(*args)


def upsample_kernel(halo_ref, block_ref, w_ref, bias_ref, out_ref):
    t = pl.program_id(0)
    s = pl.program_id(1)
    cells = RH * WD
    halo = [halo_ref[i].reshape(cells, CH) for i in range(FT)]
    own = [block_ref[i].reshape(cells, CH) for i in range(FT)]

    def emit(parts):
        field = jnp.concatenate(parts, axis=1)
        w = w_ref[...].reshape(3 * CH, CH)
        total = jnp.dot(field, w, preferred_element_type=F32) + bias_ref[...]
        total = total.astype(BF16).astype(F32).reshape(RH, WD, CH)
        for r in range(RH):
            wide = jnp.broadcast_to(total[r][:, None, :], (WD, 2, CH)).reshape(2 * WD, CH).astype(BF16)
            out_ref[0, 2 * r] = wide
            out_ref[0, 2 * r + 1] = wide

    @pl.when(t == 0)
    def _():
        emit([halo[0], halo[1], own[0]])

    @pl.when(t == 1)
    def _():
        emit([halo[1], own[0], own[1]])


def upsample(halo, block, weight, bias):
    return pl.pallas_call(
        upsample_kernel,
        grid=(FT, 2),
        in_specs=[
            pl.BlockSpec((FT, RH, WD, CH), lambda t, s: (0, 0, 0, 0)),
            pl.BlockSpec((FT, RH, WD, CH), lambda t, s: (0, 0, 0, 0)),
            pl.BlockSpec((3, CH, CH), lambda t, s: (0, 0, s)),
            pl.BlockSpec((1, CH), lambda t, s: (0, s)),
        ],
        out_specs=pl.BlockSpec((1, 2 * RH, 2 * WD, CH), lambda t, s: (2 * t + s, 0, 0, 0)),
        out_shape=jax.ShapeDtypeStruct((2 * FT, 2 * RH, 2 * WD, CH), BF16),
        compiler_params=pltpu.CompilerParams(vmem_limit_bytes=LIMIT),
        cost_estimate=pl.CostEstimate(flops=3 * 10**9, bytes_accessed=12 * 10**6, transcendentals=0),
        name="upsample",
    )(halo, block, weight, bias)


def place_kernel(tokens_ref, line_ref, column_ref, out_ref):
    tokens = tokens_ref[...]
    line = line_ref[...]
    lines = out_ref.shape[0] * RH
    count = tokens.shape[1]
    zero = jnp.zeros_like(tokens)
    column = lax.broadcasted_iota(jnp.int32, (128, count), 0) == column_ref[...]
    column = column.astype(F32).astype(BF16)
    for t in range(FT):
        rows = [jnp.where(line == t * lines + h, tokens, zero) for h in range(lines)]
        placed = lax.dot_general(jnp.concatenate(rows, axis=0), column, NT, preferred_element_type=F32)
        placed = placed.astype(BF16).reshape(lines, ZC, 128)
        for g in range(out_ref.shape[0]):
            first = RH * g - 2
            for i in range(RH + 4):
                if 0 <= first + i < lines:
                    out_ref[g, t, i] = placed[first + i]
                else:
                    out_ref[g, t, i] = jnp.zeros((ZC, 128), BF16)


def latent_field(tokens, token_pos):
    tiles = lax.axis_size("height")
    slab = lax.axis_index("frame")
    count = tokens.shape[1]
    places = lax.dynamic_slice_in_dim(token_pos, lax.axis_index("height") * count, count, 0)
    line = places // WD - slab * (FT * RH * tiles)
    column = places % WD + 1
    grids = pl.pallas_call(
        place_kernel,
        in_specs=[VMEM] * 3,
        out_specs=VMEM,
        out_shape=jax.ShapeDtypeStruct((tiles, FT, RH + 4, ZC, 128), BF16),
        compiler_params=pltpu.CompilerParams(vmem_limit_bytes=LIMIT),
        cost_estimate=pl.CostEstimate(flops=3 * 10**8, bytes_accessed=10**6, transcendentals=0),
        name="place_tokens",
    )(tokens, line.reshape(1, count), column.reshape(1, count))
    grids = lax.all_to_all(grids, "height", 0, 0, tiled=True)
    own = jnp.sum(grids.astype(F32), axis=0).astype(BF16)
    return along(own, "frame", 2), along(own, "frame", 1), own


def on_device(
    tokens,
    token_pos,
    weight_in,
    bias_in,
    gain_one,
    offset_one,
    weight_one,
    bias_one,
    gain_two,
    offset_two,
    weight_two,
    bias_two,
    weight_time,
    bias_time,
):
    devices = lax.axis_size("frame") * lax.axis_size("height")
    slab, tile = lax.axis_index("frame"), lax.axis_index("height")
    side = 4
    in_x, in_y = slab % side, slab // side
    place = jnp.stack([tile // 2, tile % 2, in_x, in_y]).astype(jnp.int32)

    def send_x(v, k):
        return lax.ppermute(v, "frame", [(side * y + x, side * y + (x + k) % side) for y in range(4) for x in range(4)])

    def send_y(v, k):
        return lax.ppermute(v, "frame", [(side * y + x, side * ((y + k) % side) + x) for y in range(4) for x in range(4)])

    def unit_of(weight, low, high):
        unit = jnp.transpose(weight[:, :, low:high], (2, 0, 1, 4, 3))
        return unit.reshape(-1, 3, unit.shape[3], CH)

    def gathered(weight, low, high):
        return lax.all_gather(jnp.swapaxes(weight[:, :, low:high], 3, 4), "height", axis=3, tiled=True)

    def plan_of(low, high):
        return [(0, e - low, 3, e, 0, CH, None) for e in range(low, high)]

    rest, plan = ring_plan(*ring_gather(unit_of(weight_one, 2, 3), send_x, in_x), [2], 2, 1)
    kernel_one = ([gathered(weight_one, 0, 2), *rest], plan_of(0, 2) + plan)
    rest, plan = ring_plan(*ring_gather(unit_of(weight_two, 1, 3), send_y, in_y), [1, 2], 3, 1)
    kernel_two = ([gathered(weight_two, 0, 1), *rest], plan_of(0, 1) + plan)
    flags = jnp.stack([slab > 0, tile > 0, tile < lax.axis_size("height") - 1]).astype(F32)
    row = lambda v: v.reshape(1, -1)

    latent = latent_field(tokens, token_pos)
    base, stat = input_conv(latent, weight_in.reshape(-1, CH), row(bias_in), devices)

    def edges(j):
        return [1] if j == 0 else [2] if j == RH + 1 else []

    everything = lambda i, j: ([0] if i < FT else []) + edges(j)
    inner, stat = block_conv(
        "conv_one",
        [base],
        [(0, 2 * FT, 0, RH + 2, everything)],
        [(t, t + a, a) for t in range(FT) for a in range(3)],
        share_stats(stat),
        flags,
        place,
        row(gain_one),
        row(offset_one),
        kernel_one,
        {"bias": row(bias_one), "stat": None},
        BF16,
        devices,
    )
    behind = along(inner, "frame", 1)
    shared = share_stats(stat)

    def rows_around(v):
        return [along(v[:, RH - 1 :], "height", 1), v, along(v[:, :1], "height", -1)]

    pieces = lambda more: [
        (0, FT, 0, 1, lambda i, j: more + [1]),
        (0, FT, 1, RH, lambda i, j: more),
        (0, FT, RH + 1, 1, lambda i, j: more + [2]),
    ]
    (partial,) = block_conv(
        "conv_two_own",
        rows_around(inner),
        pieces([]),
        [(0, 0, 2), (1, 0, 1), (1, 1, 2)],
        shared,
        flags,
        place,
        row(gain_two),
        row(offset_two),
        kernel_two,
        {},
        F32,
        devices,
    )
    (block,) = block_conv(
        "conv_two_behind",
        rows_around(behind),
        pieces([0]),
        [(0, 0, 0), (0, 1, 1), (1, 1, 0)],
        shared,
        flags,
        place,
        row(gain_two),
        row(offset_two),
        kernel_two,
        {"partial": partial, "bias": row(bias_two), "base": base},
        BF16,
        devices,
    )
    return upsample(along(block, "frame", 1), block, weight_time, row(bias_time))


def solution(mesh):
    placed = (
        P(None, ("frame", "height")),
        P("frame"),
        P(),
        P(),
        P(),
        P(),
        P(None, None, None, None, "height"),
        P(),
        P(),
        P(),
        P(None, None, None, None, "height"),
        P(),
        P(),
        P(),
    )
    return jax.shard_map(
        on_device,
        mesh=mesh,
        in_specs=placed,
        out_specs=P("frame", "height", None, None),
        check_vma=False,
    )
```

profile of v0, /device:TPU:40, one launch (start us, length us, event | category | flops | bytes accessed | tf_op | source)
XLA Modules:
  0.0 267.3 jit_solution(15766363985152395332)
XLA Ops:
  6.5 2.5 slice_bitcast_fusion.1
  11.1 1.9 collective-permute-start.2
  13.2 3.0 %collective-permute-start.4 = (bf16[3,3,16,512]{3,2,1,0:T(8,128)(2,1)}, bf16[3,3,16,512]{3,2,1,0:T(8,128)(2,1)}, u32[]{:S(2)}, u32[]{:S(2)}) collective-permute-start(bf16[3,3,16,512]{3,2,1,0:T(8,128)(2,1)} %dynamic-slice_bitcast_fusion), channel_id=1, source_target_pairs={{0,4},{1,5},{2,6},{3,7},{4,0},{5,1},{6,2},{7,3},{8,12},{9,13},{10,... | collective-permute-start | bytes 442376 | tf_op jit(solution)/shard_map/ppermute | solution.py:110
  27.4 1.7 collective-permute-start.6
  29.2 2.1 collective-permute-start.15
  35.9 10.6 %collective-permute-done.15 = bf16[6,3,16,512]{3,2,1,0:T(8,128)(2,1)S(1)} collective-permute-done((bf16[6,3,16,512]{3,2,1,0:T(8,128)(2,1)}, bf16[6,3,16,512]{3,2,1,0:T(8,128)(2,1)S(1)}, u32[]{:S(2)}, u32[]{:S(2)}) %collective-permute-start.15) | collective-permute-done | bytes 294944 | tf_op jit(solution)/shard_map/ppermute | solution.py:110
  50.9 1.8 collective-permute-start.8
  54.3 2.4 collective-permute-done.7.refs_10_
  59.6 7.2 %collective-permute-done.16.refs_10_ = bf16[18,3,16,512]{3,2,1,0:T(8,128)(2,1)S(1)} collective-permute-done((bf16[18,3,16,512]{3,2,1,0:T(8,128)(2,1)S(1)}, bf16[18,3,16,512]{3,2,1,0:T(8,128)(2,1)S(1)}, u32[]{:S(2)}, u32[]{:S(2)}) %collective-permute-start.16) | collective-permute-done | bytes 884768 | tf_op jit(solution)/shard_map/ppermute | solution.py:355
  71.7 3.5 %collective-permute-done.18.refs_12_ = bf16[9,3,16,512]{3,2,1,0:T(8,128)(2,1)S(1)} collective-permute-done((bf16[9,3,16,512]{3,2,1,0:T(8,128)(2,1)S(1)}, bf16[9,3,16,512]{3,2,1,0:T(8,128)(2,1)S(1)}, u32[]{:S(2)}, u32[]{:S(2)}) %collective-permute-start.18) | collective-permute-done | bytes 442400 | tf_op jit(solution)/shard_map/ppermute | solution.py:355
  84.0 2.2 place_tokens.1
  86.2 4.7 %all-to-all-start = ((bf16[8,2,8,16,128]{4,3,2,1,0:T(8,128)(2,1)}), bf16[8,2,8,16,128]{4,3,2,1,0:T(8,128)(2,1)S(1)}, u32[]{:S(2)}, u32[]{:S(2)}) async-start(bf16[8,2,8,16,128]{4,3,2,1,0:T(8,128)(2,1)} %place_tokens.1), calls=%async_computation | async-start | bytes 1048576 | tf_op jit(solution)/shard_map/all_to_all | solution.py:324
  90.9 14.9 %all-to-all-done = bf16[8,2,8,16,128]{4,3,2,1,0:T(8,128)(2,1)S(1)} async-done(((bf16[8,2,8,16,128]{4,3,2,1,0:T(8,128)(2,1)}), bf16[8,2,8,16,128]{4,3,2,1,0:T(8,128)(2,1)S(1)}, u32[]{:S(2)}, u32[]{:S(2)}) %all-to-all-start) | async-done | bytes 524320 | tf_op jit(solution)/shard_map/all_to_all | solution.py:324
  105.8 4.4 %collective-permute-start = (bf16[2,8,16,128]{3,2,1,0:T(8,128)(2,1)S(1)}, bf16[2,8,16,128]{3,2,1,0:T(8,128)(2,1)S(1)}, u32[]{:S(2)}, u32[]{:S(2)}) collective-permute-start(bf16[2,8,16,128]{3,2,1,0:T(8,128)(2,1)S(1)} %reduce_sum.12.own_ref), channel_id=1, source_target_pairs={{0,16},{8,24},{16,32},{24,40},{32,48},{40,56},{48,64},{56,72},{64,... | collective-permute-start | bytes 196616 | tf_op jit(solution)/shard_map/ppermute | solution.py:32
  110.3 2.5 collective-permute-start.1
  114.4 4.2 %collective-permute-done.1.behind_ref = bf16[2,8,16,128]{3,2,1,0:T(8,128)(2,1)S(1)} collective-permute-done((bf16[2,8,16,128]{3,2,1,0:T(8,128)(2,1)S(1)}, bf16[2,8,16,128]{3,2,1,0:T(8,128)(2,1)S(1)}, u32[]{:S(2)}, u32[]{:S(2)}) %collective-permute-start.1) | collective-permute-done | bytes 65568 | tf_op jit(solution)/shard_map/ppermute | solution.py:32
  119.2 4.9 %input_conv.1 = (bf16[4,6,104,512]{3,2,1,0:T(8,128)(2,1)}, f32[128,128]{1,0:T(8,128)}) custom-call(bf16[2,8,16,128]{3,2,1,0:T(8,128)(2,1)} %copy-done.22, bf16[2,8,16,128]{3,2,1,0:T(8,128)(2,1)} %copy-done.23, bf16[2,8,16,128]{3,2,1,0:T(8,128)(2,1)} %copy-done.16, bf16[432,512]{1,0:T(8,128)(2,1)} %bitcast.55, f32[1,512]{1,0:T(1,128)} %bitcast.56), custom_call_target="tpu_custom_call" | custom-call | flops 3000000000 | bytes 4000000 | tf_op jit(solution)/shard_map/input_conv/pallas_call | solution.py:91
  124.1 6.6 %all-to-all-start.1 = ((f32[128,1,128]{2,1,0:T(1,128)}), f32[128,1,128]{2,1,0:T(1,128)S(1)}, u32[]{:S(2)}, u32[]{:S(2)}) async-start(f32[128,1,128]{2,1,0:T(1,128)} %bitcast.53), calls=%async_computation.1 | async-start | bytes 131072 | tf_op jit(solution)/shard_map/all_to_all | solution.py:66
  131.3 7.1 %all-to-all-done.1 = f32[128,1,128]{2,1,0:T(1,128)S(1)} async-done(((f32[128,1,128]{2,1,0:T(1,128)}), f32[128,1,128]{2,1,0:T(1,128)S(1)}, u32[]{:S(2)}, u32[]{:S(2)}) %all-to-all-start.1) | async-done | bytes 65568 | tf_op jit(solution)/shard_map/all_to_all | solution.py:66
  139.0 19.7 %conv_one.1 = (bf16[2,4,104,512]{3,2,1,0:T(8,128)(2,1)}, f32[128,128]{1,0:T(8,128)}) custom-call(bf16[4,6,104,512]{3,2,1,0:T(8,128)(2,1)} %get-tuple-element.9.refs_0_.refs_18_, f32[128,128]{1,0:T(8,128)} %bitcast.52, f32[3]{0:T(128)} %add_convert_fusion.refs_2_.refs_4_, s32[4]{0:T(128)} %pad_add_fusion.refs_3_.refs_5_, f32[1,512]{1,0:T(1,128)} %bitcast.57, ...), custom_call_target="tpu_custom_call" | custom-call | flops 12683575296 | bytes 16000000 | tf_op jit(solution)/shard_map/conv_one/pallas_call | solution.py:224
  158.7 2.4 collective-permute-start.10
  161.1 8.3 %all-to-all-start.2 = ((f32[128,1,128]{2,1,0:T(1,128)}), f32[128,1,128]{2,1,0:T(1,128)S(1)}, u32[]{:S(2)}, u32[]{:S(2)}) async-start(f32[128,1,128]{2,1,0:T(1,128)} %bitcast.51), calls=%async_computation.2 | async-start | bytes 131072 | tf_op jit(solution)/shard_map/all_to_all | solution.py:66
  170.5 2.1 collective-permute-start.21
  172.6 3.5 %collective-permute-start.22 = (bf16[2,1,104,512]{3,2,1,0:T(8,128)(2,1)S(1)}, bf16[2,1,104,512]{3,2,1,0:T(8,128)(2,1)S(1)}, u32[]{:S(2)}, u32[]{:S(2)}) collective-permute-start(bf16[2,1,104,512]{3,2,1,0:T(8,128)(2,1)S(1)} %get-tuple-element.15), channel_id=1, source_target_pairs={{1,0},{2,1},{3,2},{4,3},{5,4},{6,5},{7,6},{9,8},{10,9},{11,10},{12... | collective-permute-start | bytes 638984 | tf_op jit(solution)/shard_map/ppermute | solution.py:32
  176.1 8.3 %collective-permute-done.10.refs_1_ = bf16[2,4,104,512]{3,2,1,0:T(8,128)(2,1)S(1)} collective-permute-done((bf16[2,4,104,512]{3,2,1,0:T(8,128)(2,1)}, bf16[2,4,104,512]{3,2,1,0:T(8,128)(2,1)S(1)}, u32[]{:S(2)}, u32[]{:S(2)}) %collective-permute-start.10) | collective-permute-done | bytes 852000 | tf_op jit(solution)/shard_map/ppermute | solution.py:32
  184.4 1.9 collective-permute-start.11
  186.4 12.4 %collective-permute-start.12 = (bf16[2,1,104,512]{3,2,1,0:T(8,128)(2,1)S(1)}, bf16[2,1,104,512]{3,2,1,0:T(8,128)(2,1)S(1)}, u32[]{:S(2)}, u32[]{:S(2)}) collective-permute-start(bf16[2,1,104,512]{3,2,1,0:T(8,128)(2,1)S(1)} %get-tuple-element.17), channel_id=1, source_target_pairs={{1,0},{2,1},{3,2},{4,3},{5,4},{6,5},{7,6},{9,8},{10,9},{11,10},{12... | collective-permute-start | bytes 638984 | tf_op jit(solution)/shard_map/ppermute | solution.py:32
  199.6 11.4 %conv_two_own.1.refs_16_ = f32[2,4,104,512]{3,2,1,0:T(8,128)} custom-call(bf16[2,1,104,512]{3,2,1,0:T(8,128)(2,1)} %copy-done.20, bf16[2,4,104,512]{3,2,1,0:T(8,128)(2,1)} %get-tuple-element.11.refs_1_, bf16[2,1,104,512]{3,2,1,0:T(8,128)(2,1)} %copy-done.21, f32[128,128]{1,0:T(8,128)} %bitcast.49, f32[3]{0:T(128)} %add_convert_fusion.refs_2_.refs_4_, ...), custom_call_target="tpu_custom_call" | custom-call | flops 6341787648 | bytes 16000000 | tf_op jit(solution)/shard_map/conv_two_own/pallas_call | solution.py:224
  211.8 13.0 %conv_two_behind.1.block_ref = bf16[2,4,104,512]{3,2,1,0:T(8,128)(2,1)} custom-call(bf16[2,1,104,512]{3,2,1,0:T(8,128)(2,1)} %copy-done.18, bf16[2,4,104,512]{3,2,1,0:T(8,128)(2,1)} %copy-done.11, bf16[2,1,104,512]{3,2,1,0:T(8,128)(2,1)} %copy-done.19, f32[128,128]{1,0:T(8,128)} %bitcast.50, f32[3]{0:T(128)} %add_convert_fusion.refs_2_.refs_4_, ...), custom_call_target="tpu_custom_call" | custom-call | flops 6341787648 | bytes 16000000 | tf_op jit(solution)/shard_map/conv_two_behind/pallas_call | solution.py:224
  224.8 1.9 collective-permute-start.23
  226.7 22.2 %collective-permute-done.23.halo_ref = bf16[2,4,104,512]{3,2,1,0:T(8,128)(2,1)S(1)} collective-permute-done((bf16[2,4,104,512]{3,2,1,0:T(8,128)(2,1)}, bf16[2,4,104,512]{3,2,1,0:T(8,128)(2,1)S(1)}, u32[]{:S(2)}, u32[]{:S(2)}) %collective-permute-start.23) | collective-permute-done | bytes 852000 | tf_op jit(solution)/shard_map/ppermute | solution.py:32
  249.9 10.3 %upsample.1 = bf16[4,8,208,512]{3,2,1,0:T(8,128)(2,1)} custom-call(bf16[2,4,104,512]{3,2,1,0:T(8,128)(2,1)} %copy-done.7, bf16[2,4,104,512]{3,2,1,0:T(8,128)(2,1)} %conv_two_behind.1.block_ref, bf16[3,512,1024]{2,1,0:T(8,128)(2,1)} %w_ref.1, f32[1,1024]{1,0:T(1,128)} %bitcast.54), custom_call_target="tpu_custom_call" | custom-call | flops 3000000000 | bytes 12000000 | tf_op jit(solution)/shard_map/upsample/pallas_call | solution.py:270
  (123 shorter events, 47.5 us)
Async XLA Ops:
  6.5 131.8 %all-gather.3.cloned.1.call-start = ((), (), s32[]{:S(2)}) async-start(), calls=%async_computation.3 | async-start | bytes 10616832 | tf_op jit(solution)/shard_map/all_gather | solution.py:362
  9.1 189.7 %all-gather.5.cloned.1.call-start = ((), (), s32[]{:S(2)}) async-start(), calls=%async_computation.4 | async-start | bytes 5308416 | tf_op jit(solution)/shard_map/all_gather | solution.py:362
  10.4 70.5 %copy-start.1 = (bf16[3,3,64,512]{3,2,1,0:T(8,128)(2,1)}, bf16[3,3,64,512]{3,2,1,0:T(8,128)(2,1)S(1)}, u32[]{:S(2)}) copy-start(bf16[3,3,64,512]{3,2,1,0:T(8,128)(2,1)S(1)} %get-tuple-element.13.refs_12_) | copy-start | bytes 1769476
  11.1 9.0 %collective-permute-start.2 = (bf16[3,3,16,512]{3,2,1,0:T(8,128)(2,1)}, bf16[3,3,16,512]{3,2,1,0:T(8,128)(2,1)}, u32[]{:S(2)}, u32[]{:S(2)}) collective-permute-start(bf16[3,3,16,512]{3,2,1,0:T(8,128)(2,1)} %dynamic-slice_bitcast_fusion), channel_id=1, source_target_pairs={{0,2},{1,3},{2,4},{3,5},{4,6},{5,7},{6,0},{7,1},{8,10},{9,11},{10,... | collective-permute-start | bytes 442376 | tf_op jit(solution)/shard_map/ppermute | solution.py:110
  13.0 8.7 %collective-permute-start.3 = (bf16[3,3,16,512]{3,2,1,0:T(8,128)(2,1)}, bf16[3,3,16,512]{3,2,1,0:T(8,128)(2,1)}, u32[]{:S(2)}, u32[]{:S(2)}) collective-permute-start(bf16[3,3,16,512]{3,2,1,0:T(8,128)(2,1)} %dynamic-slice_bitcast_fusion), channel_id=1, source_target_pairs={{0,6},{1,7},{2,0},{3,1},{4,2},{5,3},{6,4},{7,5},{8,14},{9,15},{10,... | collective-permute-start | bytes 442376 | tf_op jit(solution)/shard_map/ppermute | solution.py:110
  13.2 11.2 %collective-permute-start.4 = (bf16[3,3,16,512]{3,2,1,0:T(8,128)(2,1)}, bf16[3,3,16,512]{3,2,1,0:T(8,128)(2,1)}, u32[]{:S(2)}, u32[]{:S(2)}) collective-permute-start(bf16[3,3,16,512]{3,2,1,0:T(8,128)(2,1)} %dynamic-slice_bitcast_fusion), channel_id=1, source_target_pairs={{0,4},{1,5},{2,6},{3,7},{4,0},{5,1},{6,2},{7,3},{8,12},{9,13},{10,... | collective-permute-start | bytes 442376 | tf_op jit(solution)/shard_map/ppermute | solution.py:110
  16.3 63.8 %copy-start = (bf16[2,3,3,64,512]{4,3,2,1,0:T(8,128)(2,1)}, bf16[2,3,3,64,512]{4,3,2,1,0:T(8,128)(2,1)S(1)}, u32[]{:S(2)}) copy-start(bf16[2,3,3,64,512]{4,3,2,1,0:T(8,128)(2,1)S(1)} %copy.20) | copy-start | bytes 3538948
  17.1 15.3 %collective-permute-start.13 = (bf16[6,3,16,512]{3,2,1,0:T(8,128)(2,1)}, bf16[6,3,16,512]{3,2,1,0:T(8,128)(2,1)}, u32[]{:S(2)}, u32[]{:S(2)}) collective-permute-start(bf16[6,3,16,512]{3,2,1,0:T(8,128)(2,1)} %constant_dynamic-slice_fusion), channel_id=1, source_target_pairs={{0,2},{1,3},{2,4},{3,5},{4,6},{5,7},{6,0},{7,1},{8,10},{9,11},{10,... | collective-permute-start | bytes 884744 | tf_op jit(solution)/shard_map/ppermute | solution.py:110
  17.8 16.4 %collective-permute-start.14 = (bf16[6,3,16,512]{3,2,1,0:T(8,128)(2,1)}, bf16[6,3,16,512]{3,2,1,0:T(8,128)(2,1)}, u32[]{:S(2)}, u32[]{:S(2)}) collective-permute-start(bf16[6,3,16,512]{3,2,1,0:T(8,128)(2,1)} %constant_dynamic-slice_fusion), channel_id=1, source_target_pairs={{0,6},{1,7},{2,0},{3,1},{4,2},{5,3},{6,4},{7,5},{8,14},{9,15},{10,... | collective-permute-start | bytes 884744 | tf_op jit(solution)/shard_map/ppermute | solution.py:110
  25.9 28.4 %copy-start.17 = (bf16[9,3,16,512]{3,2,1,0:T(8,128)(2,1)}, bf16[9,3,16,512]{3,2,1,0:T(8,128)(2,1)S(1)}, u32[]{:S(2)}) copy-start(bf16[9,3,16,512]{3,2,1,0:T(8,128)(2,1)S(1)} %get-tuple-element.26.refs_7_) | copy-start | bytes 1327108
  26.0 23.3 %collective-permute-start.5 = (bf16[9,3,16,512]{3,2,1,0:T(8,128)(2,1)S(1)}, bf16[9,3,16,512]{3,2,1,0:T(8,128)(2,1)S(1)}, u32[]{:S(2)}, u32[]{:S(2)}) collective-permute-start(bf16[9,3,16,512]{3,2,1,0:T(8,128)(2,1)S(1)} %get-tuple-element.26.refs_7_), channel_id=1, source_target_pairs={{0,8},{8,16},{16,24},{24,0},{32,40},{40,48},{48,56},{56,32},{64,72... | collective-permute-start | bytes 1327112 | tf_op jit(solution)/shard_map/ppermute | solution.py:352
  27.4 23.4 %collective-permute-start.6 = (bf16[9,3,16,512]{3,2,1,0:T(8,128)(2,1)S(1)}, bf16[9,3,16,512]{3,2,1,0:T(8,128)(2,1)S(1)}, u32[]{:S(2)}, u32[]{:S(2)}) collective-permute-start(bf16[9,3,16,512]{3,2,1,0:T(8,128)(2,1)S(1)} %get-tuple-element.26.refs_7_), channel_id=1, source_target_pairs={{0,24},{8,0},{16,8},{24,16},{32,56},{40,32},{48,40},{56,48},{64,88... | collective-permute-start | bytes 1327112 | tf_op jit(solution)/shard_map/ppermute | solution.py:352
  29.2 17.3 %collective-permute-start.15 = (bf16[6,3,16,512]{3,2,1,0:T(8,128)(2,1)}, bf16[6,3,16,512]{3,2,1,0:T(8,128)(2,1)S(1)}, u32[]{:S(2)}, u32[]{:S(2)}) collective-permute-start(bf16[6,3,16,512]{3,2,1,0:T(8,128)(2,1)} %constant_dynamic-slice_fusion), channel_id=1, source_target_pairs={{0,4},{1,5},{2,6},{3,7},{4,0},{5,1},{6,2},{7,3},{8,12},{9,13},{10,... | collective-permute-start | bytes 884744 | tf_op jit(solution)/shard_map/ppermute | solution.py:110
  47.2 19.6 %collective-permute-start.16 = (bf16[18,3,16,512]{3,2,1,0:T(8,128)(2,1)S(1)}, bf16[18,3,16,512]{3,2,1,0:T(8,128)(2,1)S(1)}, u32[]{:S(2)}, u32[]{:S(2)}) collective-permute-start(bf16[18,3,16,512]{3,2,1,0:T(8,128)(2,1)S(1)} %get-tuple-element.20.refs_9_), channel_id=1, source_target_pairs={{0,32},{8,40},{16,48},{24,56},{32,64},{40,72},{48,80},{56,88},{64,... | collective-permute-start | bytes 2654216 | tf_op jit(solution)/shard_map/ppermute | solution.py:355
  48.9 19.7 %collective-permute-start.17 = (bf16[18,3,16,512]{3,2,1,0:T(8,128)(2,1)S(1)}, bf16[18,3,16,512]{3,2,1,0:T(8,128)(2,1)S(1)}, u32[]{:S(2)}, u32[]{:S(2)}) collective-permute-start(bf16[18,3,16,512]{3,2,1,0:T(8,128)(2,1)S(1)} %get-tuple-element.20.refs_9_), channel_id=1, source_target_pairs={{0,96},{8,104},{16,112},{24,120},{32,0},{40,8},{48,16},{56,24},{64... | collective-permute-start | bytes 2654216 | tf_op jit(solution)/shard_map/ppermute | solution.py:355
  49.3 7.5 %collective-permute-start.7 = (bf16[5,3,16,512]{3,2,1,0:T(8,128)(2,1)S(1)}, bf16[5,3,16,512]{3,2,1,0:T(8,128)(2,1)S(1)}, u32[]{:S(2)}, u32[]{:S(2)}) collective-permute-start(bf16[5,3,16,512]{3,2,1,0:T(8,128)(2,1)S(1)} %slice.80), channel_id=1, source_target_pairs={{0,8},{8,16},{16,24},{24,0},{32,40},{40,48},{48,56},{56,32},{64,72... | collective-permute-start | bytes 737288 | tf_op jit(solution)/shard_map/ppermute | solution.py:352
  50.9 6.6 %collective-permute-start.8 = (bf16[4,3,16,512]{3,2,1,0:T(8,128)(2,1)S(1)}, bf16[4,3,16,512]{3,2,1,0:T(8,128)(2,1)S(1)}, u32[]{:S(2)}, u32[]{:S(2)}) collective-permute-start(bf16[4,3,16,512]{3,2,1,0:T(8,128)(2,1)S(1)} %slice.81), channel_id=1, source_target_pairs={{0,24},{8,0},{16,8},{24,16},{32,56},{40,32},{48,40},{56,48},{64,88... | collective-permute-start | bytes 589832 | tf_op jit(solution)/shard_map/ppermute | solution.py:352
  66.9 8.4 %collective-permute-start.18 = (bf16[9,3,16,512]{3,2,1,0:T(8,128)(2,1)S(1)}, bf16[9,3,16,512]{3,2,1,0:T(8,128)(2,1)S(1)}, u32[]{:S(2)}, u32[]{:S(2)}) collective-permute-start(bf16[9,3,16,512]{3,2,1,0:T(8,128)(2,1)S(1)} %slice.88), channel_id=1, source_target_pairs={{0,32},{8,40},{16,48},{24,56},{32,64},{40,72},{48,80},{56,88},{64,... | collective-permute-start | bytes 1327112 | tf_op jit(solution)/shard_map/ppermute | solution.py:355
  68.6 8.4 %collective-permute-start.19 = (bf16[9,3,16,512]{3,2,1,0:T(8,128)(2,1)S(1)}, bf16[9,3,16,512]{3,2,1,0:T(8,128)(2,1)S(1)}, u32[]{:S(2)}, u32[]{:S(2)}) collective-permute-start(bf16[9,3,16,512]{3,2,1,0:T(8,128)(2,1)S(1)} %slice.89), channel_id=1, source_target_pairs={{0,96},{8,104},{16,112},{24,120},{32,0},{40,8},{48,16},{56,24},{64... | collective-permute-start | bytes 1327112 | tf_op jit(solution)/shard_map/ppermute | solution.py:355
  80.8 117.9 %collective-permute-start.20 = (bf16[96,3,16,512]{3,2,1,0:T(8,128)(2,1)}, bf16[96,3,16,512]{3,2,1,0:T(8,128)(2,1)}, u32[]{:S(2)}, u32[]{:S(2)}) collective-permute-start(bf16[96,3,16,512]{3,2,1,0:T(8,128)(2,1)} %slice_dynamic-update-slice_fusion), channel_id=1, source_target_pairs={{0,1},{1,0},{2,3},{3,2},{4,5},{5,4},{6,7},{7,6},{8,9},{9,8},{10,11... | collective-permute-start | bytes 14155784 | tf_op jit(solution)/shard_map/ppermute | solution.py:116
  81.5 56.8 %collective-permute-start.9 = (bf16[48,3,16,512]{3,2,1,0:T(8,128)(2,1)}, bf16[48,3,16,512]{3,2,1,0:T(8,128)(2,1)}, u32[]{:S(2)}, u32[]{:S(2)}) collective-permute-start(bf16[48,3,16,512]{3,2,1,0:T(8,128)(2,1)} %slice_dynamic-update-slice_fusion.4), channel_id=1, source_target_pairs={{0,1},{1,0},{2,3},{3,2},{4,5},{5,4},{6,7},{7,6},{8,9},{9,8},{10,11... | collective-permute-start | bytes 7077896 | tf_op jit(solution)/shard_map/ppermute | solution.py:116
  86.2 19.6 %all-to-all-start = ((bf16[8,2,8,16,128]{4,3,2,1,0:T(8,128)(2,1)}), bf16[8,2,8,16,128]{4,3,2,1,0:T(8,128)(2,1)S(1)}, u32[]{:S(2)}, u32[]{:S(2)}) async-start(bf16[8,2,8,16,128]{4,3,2,1,0:T(8,128)(2,1)} %place_tokens.1), calls=%async_computation | async-start | bytes 1048576 | tf_op jit(solution)/shard_map/all_to_all | solution.py:324
  105.8 8.6 %collective-permute-start = (bf16[2,8,16,128]{3,2,1,0:T(8,128)(2,1)S(1)}, bf16[2,8,16,128]{3,2,1,0:T(8,128)(2,1)S(1)}, u32[]{:S(2)}, u32[]{:S(2)}) collective-permute-start(bf16[2,8,16,128]{3,2,1,0:T(8,128)(2,1)S(1)} %reduce_sum.12.own_ref), channel_id=1, source_target_pairs={{0,16},{8,24},{16,32},{24,40},{32,48},{40,56},{48,64},{56,72},{64,... | collective-permute-start | bytes 196616 | tf_op jit(solution)/shard_map/ppermute | solution.py:32
  110.3 8.3 %collective-permute-start.1 = (bf16[2,8,16,128]{3,2,1,0:T(8,128)(2,1)S(1)}, bf16[2,8,16,128]{3,2,1,0:T(8,128)(2,1)S(1)}, u32[]{:S(2)}, u32[]{:S(2)}) collective-permute-start(bf16[2,8,16,128]{3,2,1,0:T(8,128)(2,1)S(1)} %reduce_sum.12.own_ref), channel_id=1, source_target_pairs={{0,8},{8,16},{16,24},{24,32},{32,40},{40,48},{48,56},{56,64},{64,7... | collective-permute-start | bytes 196616 | tf_op jit(solution)/shard_map/ppermute | solution.py:32
  124.1 14.3 %all-to-all-start.1 = ((f32[128,1,128]{2,1,0:T(1,128)}), f32[128,1,128]{2,1,0:T(1,128)S(1)}, u32[]{:S(2)}, u32[]{:S(2)}) async-start(f32[128,1,128]{2,1,0:T(1,128)} %bitcast.53), calls=%async_computation.1 | async-start | bytes 131072 | tf_op jit(solution)/shard_map/all_to_all | solution.py:66
  158.7 25.7 %collective-permute-start.10 = (bf16[2,4,104,512]{3,2,1,0:T(8,128)(2,1)}, bf16[2,4,104,512]{3,2,1,0:T(8,128)(2,1)S(1)}, u32[]{:S(2)}, u32[]{:S(2)}) collective-permute-start(bf16[2,4,104,512]{3,2,1,0:T(8,128)(2,1)} %get-tuple-element.11.refs_1_), channel_id=1, source_target_pairs={{0,8},{8,16},{16,24},{24,32},{32,40},{40,48},{48,56},{56,64},{64,7... | collective-permute-start | bytes 2555912 | tf_op jit(solution)/shard_map/ppermute | solution.py:32
  161.1 37.7 %all-to-all-start.2 = ((f32[128,1,128]{2,1,0:T(1,128)}), f32[128,1,128]{2,1,0:T(1,128)S(1)}, u32[]{:S(2)}, u32[]{:S(2)}) async-start(f32[128,1,128]{2,1,0:T(1,128)} %bitcast.51), calls=%async_computation.2 | async-start | bytes 131072 | tf_op jit(solution)/shard_map/all_to_all | solution.py:66
  170.5 28.3 %collective-permute-start.21 = (bf16[2,1,104,512]{3,2,1,0:T(8,128)(2,1)S(1)}, bf16[2,1,104,512]{3,2,1,0:T(8,128)(2,1)S(1)}, u32[]{:S(2)}, u32[]{:S(2)}) collective-permute-start(bf16[2,1,104,512]{3,2,1,0:T(8,128)(2,1)S(1)} %get-tuple-element.16), channel_id=1, source_target_pairs={{0,1},{1,2},{2,3},{3,4},{4,5},{5,6},{6,7},{8,9},{9,10},{10,11},{11... | collective-permute-start | bytes 638984 | tf_op jit(solution)/shard_map/ppermute | solution.py:32
  172.6 26.3 %collective-permute-start.22 = (bf16[2,1,104,512]{3,2,1,0:T(8,128)(2,1)S(1)}, bf16[2,1,104,512]{3,2,1,0:T(8,128)(2,1)S(1)}, u32[]{:S(2)}, u32[]{:S(2)}) collective-permute-start(bf16[2,1,104,512]{3,2,1,0:T(8,128)(2,1)S(1)} %get-tuple-element.15), channel_id=1, source_target_pairs={{1,0},{2,1},{3,2},{4,3},{5,4},{6,5},{7,6},{9,8},{10,9},{11,10},{12... | collective-permute-start | bytes 638984 | tf_op jit(solution)/shard_map/ppermute | solution.py:32
  184.4 26.6 %collective-permute-start.11 = (bf16[2,1,104,512]{3,2,1,0:T(8,128)(2,1)S(1)}, bf16[2,1,104,512]{3,2,1,0:T(8,128)(2,1)S(1)}, u32[]{:S(2)}, u32[]{:S(2)}) collective-permute-start(bf16[2,1,104,512]{3,2,1,0:T(8,128)(2,1)S(1)} %get-tuple-element.18), channel_id=1, source_target_pairs={{0,1},{1,2},{2,3},{3,4},{4,5},{5,6},{6,7},{8,9},{9,10},{10,11},{11... | collective-permute-start | bytes 638984 | tf_op jit(solution)/shard_map/ppermute | solution.py:32
  186.4 24.7 %collective-permute-start.12 = (bf16[2,1,104,512]{3,2,1,0:T(8,128)(2,1)S(1)}, bf16[2,1,104,512]{3,2,1,0:T(8,128)(2,1)S(1)}, u32[]{:S(2)}, u32[]{:S(2)}) collective-permute-start(bf16[2,1,104,512]{3,2,1,0:T(8,128)(2,1)S(1)} %get-tuple-element.17), channel_id=1, source_target_pairs={{1,0},{2,1},{3,2},{4,3},{5,4},{6,5},{7,6},{9,8},{10,9},{11,10},{12... | collective-permute-start | bytes 638984 | tf_op jit(solution)/shard_map/ppermute | solution.py:32
  224.8 24.2 %collective-permute-start.23 = (bf16[2,4,104,512]{3,2,1,0:T(8,128)(2,1)}, bf16[2,4,104,512]{3,2,1,0:T(8,128)(2,1)S(1)}, u32[]{:S(2)}, u32[]{:S(2)}) collective-permute-start(bf16[2,4,104,512]{3,2,1,0:T(8,128)(2,1)} %conv_two_behind.1.block_ref), channel_id=1, source_target_pairs={{0,8},{8,16},{16,24},{24,32},{32,40},{40,48},{48,56},{56,64},{64,7... | collective-permute-start | bytes 2555912 | tf_op jit(solution)/shard_map/ppermute | solution.py:32
  (21 other events, 169.1 us)
Sparse Core Ops, SparseCore 0:
  9.2 64.9 all-gather.2
  76.0 40.2 all-gather.4
where the time goes:
time: 272 us; the launch traced here: 267 us
  waiting for transfers between devices  84.5 us (31%)
  starting transfers between devices  71.3 us (26%)
  Pallas kernels  61.6 us (23%)
  local copies, waits for them, and re-layouts  33.9 us (12%)
  between operations  14 us (5%)
    pallas_call x3, Pallas kernels, block_conv(): pl.pallas_call(functools.partial(conv_kernel, pieces, products, taps, pla...  44.2 us
    ppermute x8, waiting for transfers between devices, along(): lax.ppermute(value, axis, [(source, source + steps) for source in range(l...  35.7 us
    ppermute x8, starting transfers between devices, along(): lax.ppermute(value, axis, [(source, source + steps) for source in range(l...  31.2 us
    unnamed x68, local copies, waits for them, and re-layouts  23.8 us
    all_to_all x2, starting transfers between devices, share_stats(): return lax.all_to_all(stat, ('frame', 'height'), 0, 0, tiled=True)  14.9 us
    all_to_all x1, waiting for transfers between devices, latent_field(): grids = lax.all_to_all(grids, 'height', 0, 0, tiled=True)  14.9 us
    ppermute x6, waiting for transfers between devices, ring_gather(): lax.ppermute(quarter, 'height', over(k))  12.7 us
    ppermute x4, waiting for transfers between devices, send_y(): lax.ppermute(v, 'frame', [(side * y + x, side * ((y + k) % side) + x) for...  11.7 us
  transfers between devices with their start and end apart: 29, of which 13 were waited for; matrix products, arithmetic and copies ran while one was open for 11% of the time, Pallas kernels for 14%

commit v1 on v0

--- a/solution.py
+++ b/solution.py
@@ -102,45 +102,47 @@
     )(*latent, weight, bias)
 
 
-def ring_gather(unit, send, pos):
-    units = unit.shape[0]
-    quarter = lax.dynamic_slice_in_dim(unit, pos * 16, 16, axis=2)
-    tiles = lax.axis_size("height")
-    over = lambda k: [(i, (i + 2 * k) % tiles) for i in range(tiles)]
-    piece = jnp.concatenate([lax.ppermute(quarter, "height", over(k)) for k in (1, 3, 2)], axis=0)
-    half = (piece.shape[0] + 1) // 2
-    left, right = send(piece, 1), send(piece, -1)
-    left2, right2 = send(left[:half], 1), send(right[half:], -1)
-    quarters = [unit[:, :, 16 * k : 16 * k + 16] for k in range(4)]
-    held = jnp.concatenate([piece, left, right, left2, right2, *quarters], axis=0)
-    other = lax.ppermute(held, "height", [(i, i ^ 1) for i in range(tiles)])
-    return [piece, left, right, left2, right2, unit, other], units, half
-
-
-def ring_plan(arrays, units, half, columns, axis, first):
-    plan = []
-    full = 3 * units
-
-    def add(array, start, low, high, flip, place):
-        index = low
-        while index < high:
-            stop = min(high, index - index % 3 + 3)
-            shift, e, a = index // units, index % units // 3, index % 3
-            z = 0 if place == "own" else (3, 1, 2)[shift]
-            plan.append((array, start + index - low, stop - index, columns[e], a, 16, (flip, z, axis, place)))
-            index = stop
-
-    for flip in (0, 1):
-        base = 0
-        for k, (low, high, ring) in enumerate([(0, full, 0), (0, full, 3), (0, full, 1), (0, half, 2), (half, full, 2)]):
-            add(first + (6 if flip else k), base if flip else 0, low, high, flip, ring)
-            base += high - low
-        for q in range(4 if flip else 1):
-            for u in range(units // 3):
-                start = (base + q * units if flip else 0) + 3 * u
-                rows = 16 if flip else 64
-                plan.append((first + (6 if flip else 5), start, 3, columns[u], 0, rows, (flip, 0, None, q)))
-    return arrays, plan
+def after(value, earlier):
+    return lax.optimization_barrier((value, earlier))[0]
+
+
+def device_groups(inside, outside):
+    sizes = {"y": 4, "x": 4, "z": 4, "c": 2}
+
+    def walk(names, fixed):
+        if not names:
+            return [(fixed["y"] * 4 + fixed["x"]) * 8 + fixed["z"] * 2 + fixed["c"]]
+        return [k for i in range(sizes[names[0]]) for k in walk(names[1:], {**fixed, names[0]: i})]
+
+    def settings(names):
+        if not names:
+            return [{}]
+        return [{**rest, names[0]: i} for i in range(sizes[names[0]]) for rest in settings(names[1:])]
+
+    return [walk(inside, fixed) for fixed in settings(outside)]
+
+
+def quarter_of(weight, low, high, pos):
+    taps = jnp.swapaxes(weight, 3, 4)
+    return lax.dynamic_slice(taps, (0, 0, low, 16 * pos, 0), (3, 3, high - low, 16, CH))
+
+
+def gather_plane(quarter):
+    return lax.all_gather(quarter, ("frame", "height"), axis_index_groups=device_groups("zxc", "y"))
+
+
+def plane_plan(array, low, high):
+    return [
+        (array, 8 * z + 2 * x + c, e - low, e, ("fixed", 2 * z + c, x))
+        for e in range(low, high)
+        for z in range(4)
+        for x in range(4)
+        for c in range(2)
+    ]
+
+
+def ring_plan(array, low, high, flip, step):
+    return [(array, z, e - low, e, (flip, z, step)) for e in range(low, high) for z in range(4)]
 
 
 def conv_kernel(pieces, products, taps, plan, weights, extras, *refs):
@@ -155,25 +157,15 @@
     stat_ref = refs.pop(0) if "stat" in extras else None
     field, wbuf, acc, sems = refs
     low, high = taps[0], taps[-1] + 1
-    z, core = place_ref[0], place_ref[1]
-    for e in range(3):
-        for array, start, length, column, a, rows, where in plan:
-            if column != e:
-                continue
-            begin, end = max(a, low), min(a + length, high)
-            if begin >= end:
-                continue
-            if where is None:
-                source = w_refs[array].at[pl.ds(begin, end - begin), :, start]
-                target = wbuf.at[e, pl.ds(begin - low, end - begin)]
-            else:
-                flip, shift, ring, step = where
-                block = lax.rem(z + shift, 4) * 2 + (1 - core if flip else core)
-                quarter = step if ring is None else lax.rem(place_ref[ring] + step, 4)
-                offset = pl.multiple_of(block * 64 + quarter * 16, 16)
-                source = w_refs[array].at[pl.ds(start + begin - a, end - begin)]
-                target = wbuf.at[e, pl.ds(begin - low, end - begin), :, pl.ds(offset, rows)]
-            pltpu.make_async_copy(source, target, sems.at[e]).start()
+    core, ring = place_ref[0], place_ref[1]
+    columns = sorted({copy[3] for copy in plan})
+    for array, index, source_e, e, (kind, block, quarter) in plan:
+        if kind != "fixed":
+            block = 2 * block + (1 - core if kind == "other" else core)
+            quarter = lax.rem(ring + quarter, 4)
+        rows = pl.multiple_of(block * 64 + quarter * 16, 16)
+        source = w_refs[array].at[index, pl.ds(low, high - low), :, source_e]
+        pltpu.make_async_copy(source, wbuf.at[columns.index(e), :, :, pl.ds(rows, 16)], sems.at[columns.index(e)]).start()
     mean, inverse = combine_stats(stats_ref, CELLS * (CH // GROUPS))
     scale = inverse * gain_ref[...]
     offset = offset_ref[...]
@@ -187,7 +179,9 @@
                     value = value * flags_ref[which]
                 field[frame + i, row + j, :WD] = value.astype(BF16)
                 field[frame + i, row + j, WD:] = jnp.zeros((WP - WD, CH), BF16)
-    for e in range(3):
+    total = jnp.zeros((FT * RH * WP, CH), F32)
+    edge = jnp.zeros((1, CH), F32)
+    for e, column in enumerate(columns):
         pltpu.make_async_copy(wbuf.at[e], wbuf.at[e], sems.at[e]).wait()
         for t in range(FT):
             terms = [(f, a) for (out, f, a) in products if out == t]
@@ -196,8 +190,13 @@
             acc[e, pl.ds(t * RH * WP, RH * WP)] = lax.dot_general(
                 jnp.concatenate(xs, axis=1), jnp.concatenate(ws, axis=1), NT, preferred_element_type=F32
             )
-    edge = jnp.zeros((1, CH), F32)
-    total = acc[1] + jnp.concatenate([edge, acc[0, :-1]], axis=0) + jnp.concatenate([acc[2, 1:], edge], axis=0)
+    for e, column in enumerate(columns):
+        if column == 0:
+            total = total + jnp.concatenate([edge, acc[e, :-1]], axis=0)
+        elif column == 1:
+            total = total + acc[e]
+        else:
+            total = total + jnp.concatenate([acc[e, 1:], edge], axis=0)
     total = total.reshape(FT, RH, WP, CH)[:, :, :WD]
     if partial_ref is not None:
         total = total + partial_ref[...]
@@ -212,6 +211,7 @@
 
 def block_conv(name, raws, pieces, products, stats, flags, place, gain, offset, weight, extras, kind, devices):
     arrays, plan = weight
+    columns = len({copy[3] for copy in plan})
     taps = sorted({a for _, _, a in products})
     frames = max(f for _, f, _ in products) + 1
     args = [*raws, stats, flags, place, gain, offset, *arrays]
@@ -228,13 +228,13 @@
         out_shape=shapes,
         scratch_shapes=[
             pltpu.VMEM((frames, RH + 2, WP, CH), BF16),
-            pltpu.VMEM((3, len(taps), 3, CH, CH), BF16),
-            pltpu.VMEM((3, FT * RH * WP, CH), F32),
-            pltpu.SemaphoreType.DMA((3,)),
+            pltpu.VMEM((columns, len(taps), 3, CH, CH), BF16),
+            pltpu.VMEM((columns, FT * RH * WP, CH), F32),
+            pltpu.SemaphoreType.DMA((columns,)),
         ],
         compiler_params=pltpu.CompilerParams(vmem_limit_bytes=LIMIT),
         cost_estimate=pl.CostEstimate(
-            flops=len(products) * 2 * 9 * RH * WP * CH * CH, bytes_accessed=16 * 10**6, transcendentals=0
+            flops=len(products) * 2 * 3 * columns * RH * WP * CH * CH, bytes_accessed=16 * 10**6, transcendentals=0
         ),
         name=name,
     )(*args)
@@ -251,9 +251,11 @@
         field = jnp.concatenate(parts, axis=1)
         w = w_ref[...].reshape(3 * CH, CH)
         total = jnp.dot(field, w, preferred_element_type=F32) + bias_ref[...]
-        total = total.astype(BF16).astype(F32).reshape(RH, WD, CH)
+        total = total.astype(BF16).reshape(RH, WD, CH)
+        twice = lax.broadcasted_iota(jnp.int32, (2 * WD, WD), 0) // 2 == lax.broadcasted_iota(jnp.int32, (2 * WD, WD), 1)
+        twice = twice.astype(F32).astype(BF16)
         for r in range(RH):
-            wide = jnp.broadcast_to(total[r][:, None, :], (WD, 2, CH)).reshape(2 * WD, CH).astype(BF16)
+            wide = jnp.dot(twice, total[r], preferred_element_type=F32).astype(BF16)
             out_ref[0, 2 * r] = wide
             out_ref[0, 2 * r + 1] = wide
 
@@ -344,57 +346,59 @@
 ):
     devices = lax.axis_size("frame") * lax.axis_size("height")
     slab, tile = lax.axis_index("frame"), lax.axis_index("height")
-    side = 4
-    in_x, in_y = slab % side, slab // side
-    place = jnp.stack([tile // 2, tile % 2, in_x, in_y]).astype(jnp.int32)
-
-    def send_x(v, k):
-        return lax.ppermute(v, "frame", [(side * y + x, side * y + (x + k) % side) for y in range(4) for x in range(4)])
-
-    def send_y(v, k):
-        return lax.ppermute(v, "frame", [(side * y + x, side * ((y + k) % side) + x) for y in range(4) for x in range(4)])
-
-    def unit_of(weight, low, high):
-        unit = jnp.transpose(weight[:, :, low:high], (2, 0, 1, 4, 3))
-        return unit.reshape(-1, 3, unit.shape[3], CH)
-
-    def gathered(weight, low, high):
-        return lax.all_gather(jnp.swapaxes(weight[:, :, low:high], 3, 4), "height", axis=3, tiled=True)
-
-    def plan_of(low, high):
-        return [(0, e - low, 3, e, 0, CH, None) for e in range(low, high)]
-
-    rest, plan = ring_plan(*ring_gather(unit_of(weight_one, 2, 3), send_x, in_x), [2], 2, 1)
-    kernel_one = ([gathered(weight_one, 0, 2), *rest], plan_of(0, 2) + plan)
-    rest, plan = ring_plan(*ring_gather(unit_of(weight_two, 1, 3), send_y, in_y), [1, 2], 3, 1)
-    kernel_two = ([gathered(weight_two, 0, 1), *rest], plan_of(0, 1) + plan)
+    in_x, in_y = slab % 4, slab // 4
+    place = jnp.stack([tile % 2, in_y]).astype(jnp.int32)
     flags = jnp.stack([slab > 0, tile > 0, tile < lax.axis_size("height") - 1]).astype(F32)
     row = lambda v: v.reshape(1, -1)
 
+    def send_y(v, k):
+        return lax.ppermute(v, "frame", [(4 * y + x, 4 * ((y + k) % 4) + x) for y in range(4) for x in range(4)])
+
+    def swap_core(v):
+        return lax.ppermute(v, "height", [(i, i ^ 1) for i in range(8)])
+
+    near = lax.all_gather(
+        quarter_of(weight_two, 1, 3, in_y), ("frame", "height"), axis_index_groups=device_groups("z", "yxc")
+    )
+    one_a = gather_plane(after(quarter_of(weight_one, 0, 2, in_x), near))
+    one_b = gather_plane(after(quarter_of(weight_one, 2, 3, in_x), near))
+    two_a = gather_plane(after(quarter_of(weight_two, 0, 1, in_x), near))
+
     latent = latent_field(tokens, token_pos)
+    near = after(near, latent[2])
+    left, right = send_y(near, 1), send_y(near, -1)
     base, stat = input_conv(latent, weight_in.reshape(-1, CH), row(bias_in), devices)
+    shared = share_stats(stat)
+    far = send_y(after(left, shared), 1)
 
     def edges(j):
         return [1] if j == 0 else [2] if j == RH + 1 else []
 
     everything = lambda i, j: ([0] if i < FT else []) + edges(j)
+    norm_one = (shared, flags, place, row(gain_one), row(offset_one))
+    common = ([base], [(0, 2 * FT, 0, RH + 2, everything)], [(t, t + a, a) for t in range(FT) for a in range(3)])
+    (partial,) = block_conv(
+        "conv_one_first", *common, *norm_one, ([one_a], plane_plan(0, 0, 2)), {}, F32, devices
+    )
+    swapped = [swap_core(after(v, shared)) for v in (near, left, right)]
     inner, stat = block_conv(
-        "conv_one",
-        [base],
-        [(0, 2 * FT, 0, RH + 2, everything)],
-        [(t, t + a, a) for t in range(FT) for a in range(3)],
-        share_stats(stat),
-        flags,
-        place,
-        row(gain_one),
-        row(offset_one),
-        kernel_one,
-        {"bias": row(bias_one), "stat": None},
+        "conv_one_last",
+        *common,
+        *norm_one,
+        ([one_b], plane_plan(0, 2, 3)),
+        {"partial": partial, "bias": row(bias_one), "stat": None},
         BF16,
         devices,
     )
+    shared = share_stats(stat)
     behind = along(inner, "frame", 1)
-    shared = share_stats(stat)
+    swapped.append(swap_core(after(far, inner)))
+    arrays = [two_a, near, left, right, far, *swapped]
+    plan = plane_plan(0, 0, 1)
+    for k, step in enumerate((0, 3, 1, 2)):
+        plan += ring_plan(1 + k, 1, 3, "own", step) + ring_plan(5 + k, 1, 3, "other", step)
+    kernel_two = (arrays, plan)
+    norm_two = (shared, flags, place, row(gain_two), row(offset_two))
 
     def rows_around(v):
         return [along(v[:, RH - 1 :], "height", 1), v, along(v[:, :1], "height", -1)]
@@ -409,11 +413,7 @@
         rows_around(inner),
         pieces([]),
         [(0, 0, 2), (1, 0, 1), (1, 1, 2)],
-        shared,
-        flags,
-        place,
-        row(gain_two),
-        row(offset_two),
+        *norm_two,
         kernel_two,
         {},
         F32,
@@ -424,11 +424,7 @@
         rows_around(behind),
         pieces([0]),
         [(0, 0, 0), (0, 1, 1), (1, 1, 0)],
-        shared,
-        flags,
-        place,
-        row(gain_two),
-        row(offset_two),
+        *norm_two,
         kernel_two,
         {"partial": partial, "bias": row(bias_two), "base": base},
         BF16,

time: 272 us -> 278 us (1.022)
  waiting for transfers between devices: 84.5 us -> 111 us
  local copies, waits for them, and re-layouts: 33.9 us -> 10.6 us
  starting transfers between devices: 71.3 us -> 51.8 us
  blocking collectives: 0 us -> 16.5 us
  Pallas kernels: 61.6 us -> 69 us
    all_gather x2 -> x4, waiting for transfers between devices: 0.02 us -> 60.8 us  [the longest x3 36.3 us: gather_plane(): lax.all_gather(quarter, ('frame', 'height'), axis_index_groups=device_gro...]
    ppermute x16 -> x7, waiting for transfers between devices: 26.9 us -> 0.02 us  [the longest x4 0.01 us: swap_core(): return lax.ppermute(v, 'height', [(i, i ^ 1) for i in range(8)])]
    unnamed x68 -> x24, local copies, waits for them, and re-layouts: 23.8 us -> 3.02 us
    all_to_all x0 -> x1, blocking collectives: none -> 16.5 us  [latent_field(): grids = lax.all_to_all(grids, 'height', 0, 0, tiled=True)]
    ppermute x16 -> x7, starting transfers between devices: 20.4 us -> 4.46 us  [the longest x3 3.38 us: send_y(): lax.ppermute(v, 'frame', [(4 * y + x, 4 * ((y + k) % 4) + x) for y in ran...]
    all_to_all x1 -> x0, waiting for transfers between devices: 14.9 us -> none  [latent_field(): grids = lax.all_to_all(grids, 'height', 0, 0, tiled=True)]
    pallas_call x3 -> x4, Pallas kernels: 44.2 us -> 53 us  [block_conv(): pl.pallas_call(functools.partial(conv_kernel, pieces, products, taps, pla...]
    ppermute x8, waiting for transfers between devices: 35.7 us -> 42.9 us  [along(): lax.ppermute(value, axis, [(source, source + steps) for source in range(l...]
  transfers between devices with their start and end apart: 29 -> 21, of which waited for: 13 -> 8; matrix products, arithmetic and copies ran while one was open for 11% -> 3% of each run, Pallas kernels for 14% -> 17%
where the time goes in v1:
time: 278 us; the launch traced here: 275 us
  waiting for transfers between devices  111 us (40%)
  Pallas kernels  69 us (25%)
  starting transfers between devices  51.8 us (19%)
  blocking collectives  16.5 us (6%)
  between operations  13.6 us (5%)
  local copies, waits for them, and re-layouts  10.6 us (4%)
    pallas_call x4, Pallas kernels, block_conv(): pl.pallas_call(functools.partial(conv_kernel, pieces, products, taps, pla...  53 us
    ppermute x8, waiting for transfers between devices, along(): lax.ppermute(value, axis, [(source, source + steps) for source in range(l...  42.9 us
    all_gather x3, waiting for transfers between devices, gather_plane(): lax.all_gather(quarter, ('frame', 'height'), axis_index_groups=device_gro...  36.3 us
    ppermute x8, starting transfers between devices, along(): lax.ppermute(value, axis, [(source, source + steps) for source in range(l...  31.8 us
    all_gather x1, waiting for transfers between devices, on_device(): lax.all_gather(quarter_of(weight_two, 1, 3, in_y), ('frame', 'height'), a...  24.5 us
    all_to_all x1, blocking collectives, latent_field(): grids = lax.all_to_all(grids, 'height', 0, 0, tiled=True)  16.5 us
    all_to_all x2, starting transfers between devices, share_stats(): return lax.all_to_all(stat, ('frame', 'height'), 0, 0, tiled=True)  15.3 us
    pallas_call x1, Pallas kernels, upsample(): pl.pallas_call(upsample_kernel, grid=(FT, 2), in_specs=[pl.BlockSpec((FT,...  8.94 us
  transfers between devices with their start and end apart: 21, of which 8 were waited for; matrix products, arithmetic and copies ran while one was open for 3% of the time, Pallas kernels for 17%

profile of v1, /device:TPU:40, one launch (start us, length us, event | category | flops | bytes accessed | tf_op | source)
XLA Modules:
  0.0 275.0 jit_solution(7411325023576805393)
XLA Ops:
  6.5 1.7 dynamic-slice_bitcast_fusion.1
  8.3 1.7 dynamic-slice_bitcast_fusion
  10.1 24.5 %all-gather.9.cloned.1.call-done = bf16[12,3,2,16,512]{4,3,2,1,0:T(8,128)(2,1)} async-done(((bf16[3,3,2,16,512]{4,3,2,1,0:T(8,128)(2,1)}), bf16[12,3,2,16,512]{4,3,2,1,0:T(8,128)(2,1)}) %all-gather.9.cloned.1.call-update) | async-done | bytes 1179664 | tf_op jit(solution)/shard_map/all_gather | solution.py:360
  34.6 1.8 dynamic-slice_bitcast_fusion.2
  39.0 2.2 place_tokens.1
  41.2 16.5 %all_to_all.27 = bf16[8,2,8,16,128]{4,3,2,1,0:T(8,128)(2,1)S(1)} all-to-all(bf16[8,2,8,16,128]{4,3,2,1,0:T(8,128)(2,1)} %place_tokens.1), channel_id=1, replica_groups=mesh['frame'=16,'height'=8] {'height'}, dimensions={0} | all-to-all | bytes 1048576 | tf_op jit(solution)/shard_map/all_to_all | solution.py:326
  57.9 1.6 collective-permute-start.5
  60.0 5.3 %collective-permute-start = (bf16[2,8,16,128]{3,2,1,0:T(8,128)(2,1)S(1)}, bf16[2,8,16,128]{3,2,1,0:T(8,128)(2,1)S(1)}, u32[]{:S(2)}, u32[]{:S(2)}) collective-permute-start(bf16[2,8,16,128]{3,2,1,0:T(8,128)(2,1)S(1)} %reduce_sum.12.own_ref), channel_id=1, source_target_pairs={{0,16},{8,24},{16,32},{24,40},{32,48},{40,56},{48,64},{56,72},{64,... | collective-permute-start | bytes 196616 | tf_op jit(solution)/shard_map/ppermute | solution.py:32
  65.3 2.5 collective-permute-start.1
  68.8 4.9 %collective-permute-done.1.behind_ref = bf16[2,8,16,128]{3,2,1,0:T(8,128)(2,1)S(1)} collective-permute-done((bf16[2,8,16,128]{3,2,1,0:T(8,128)(2,1)S(1)}, bf16[2,8,16,128]{3,2,1,0:T(8,128)(2,1)S(1)}, u32[]{:S(2)}, u32[]{:S(2)}) %collective-permute-start.1) | collective-permute-done | bytes 65568 | tf_op jit(solution)/shard_map/ppermute | solution.py:32
  74.2 4.9 %input_conv.1 = (bf16[4,6,104,512]{3,2,1,0:T(8,128)(2,1)}, f32[128,128]{1,0:T(8,128)}) custom-call(bf16[2,8,16,128]{3,2,1,0:T(8,128)(2,1)} %copy-done.10, bf16[2,8,16,128]{3,2,1,0:T(8,128)(2,1)} %copy-done.11, bf16[2,8,16,128]{3,2,1,0:T(8,128)(2,1)} %copy-done.4, bf16[432,512]{1,0:T(8,128)(2,1)} %bitcast.50, f32[1,512]{1,0:T(1,128)} %bitcast.51), custom_call_target="tpu_custom_call" | custom-call | flops 3000000000 | bytes 4000000 | tf_op jit(solution)/shard_map/input_conv/pallas_call | solution.py:91
  79.1 5.5 %all-to-all-start.1 = ((f32[128,1,128]{2,1,0:T(1,128)}), f32[128,1,128]{2,1,0:T(1,128)S(1)}, u32[]{:S(2)}, u32[]{:S(2)}) async-start(f32[128,1,128]{2,1,0:T(1,128)} %bitcast.39), calls=%async_computation.1 | async-start | bytes 131072 | tf_op jit(solution)/shard_map/all_to_all | solution.py:66
  85.3 7.0 %all-to-all-done.1 = f32[128,1,128]{2,1,0:T(1,128)S(1)} async-done(((f32[128,1,128]{2,1,0:T(1,128)}), f32[128,1,128]{2,1,0:T(1,128)S(1)}, u32[]{:S(2)}, u32[]{:S(2)}) %all-to-all-start.1) | async-done | bytes 65568 | tf_op jit(solution)/shard_map/all_to_all | solution.py:66
  92.3 1.3 collective-permute-start.7
  94.4 2.3 all-gather.13.cloned.1.call-done
  96.7 15.5 %conv_one_first.1.refs_7_ = f32[2,4,104,512]{3,2,1,0:T(8,128)} custom-call(bf16[4,6,104,512]{3,2,1,0:T(8,128)(2,1)} %get-tuple-element.17.refs_0_.refs_19_, f32[128,128]{1,0:T(8,128)} %bitcast.37, f32[3]{0:T(128)} %add_convert_fusion.refs_2_.refs_4_, s32[2]{0:T(128)} %pad_add_fusion.refs_3_.refs_5_, f32[1,512]{1,0:T(1,128)} %bitcast.52, f32[1,512]{1,0:T(1,128)} %bitcast.54, ...), custom_call_target="tpu_custom_call" | custom-call | flops 8455716864 | bytes 16000000 | tf_op jit(solution)/shard_map/conv_one_first/pallas_call | solution.py:224
  112.2 34.0 %all-gather.11.cloned.1.call-done = bf16[96,3,1,16,512]{4,3,2,1,0:T(8,128)(2,1)} async-done(((bf16[3,3,1,16,512]{4,3,2,1,0:T(8,128)(2,1)}), bf16[96,3,1,16,512]{4,3,2,1,0:T(8,128)(2,1)}) %all-gather.11.cloned.1.call-update) | async-done | bytes 4718608 | tf_op jit(solution)/shard_map/all_gather | solution.py:131
  146.2 12.0 %conv_one_last.1 = (bf16[2,4,104,512]{3,2,1,0:T(8,128)(2,1)}, f32[128,128]{1,0:T(8,128)}) custom-call(bf16[4,6,104,512]{3,2,1,0:T(8,128)(2,1)} %get-tuple-element.17.refs_0_.refs_19_, f32[128,128]{1,0:T(8,128)} %bitcast.38, f32[3]{0:T(128)} %add_convert_fusion.refs_2_.refs_4_, s32[2]{0:T(128)} %pad_add_fusion.refs_3_.refs_5_, f32[1,512]{1,0:T(1,128)} %bitcast.53, ...), custom_call_target="tpu_custom_call" | custom-call | flops 4227858432 | bytes 16000000 | tf_op jit(solution)/shard_map/conv_one_last/pallas_call | solution.py:224
  158.5 2.1 collective-permute-start.2
  160.6 9.8 %all-to-all-start.2 = ((f32[128,1,128]{2,1,0:T(1,128)}), f32[128,1,128]{2,1,0:T(1,128)S(1)}, u32[]{:S(2)}, u32[]{:S(2)}) async-start(f32[128,1,128]{2,1,0:T(1,128)} %bitcast.36), calls=%async_computation.2 | async-start | bytes 131072 | tf_op jit(solution)/shard_map/all_to_all | solution.py:66
  170.4 1.1 fusion.3
  171.5 2.1 collective-permute-start.12
  173.6 15.5 %collective-permute-done.2.refs_1_ = bf16[2,4,104,512]{3,2,1,0:T(8,128)(2,1)S(1)} collective-permute-done((bf16[2,4,104,512]{3,2,1,0:T(8,128)(2,1)}, bf16[2,4,104,512]{3,2,1,0:T(8,128)(2,1)S(1)}, u32[]{:S(2)}, u32[]{:S(2)}) %collective-permute-start.2) | collective-permute-done | bytes 852000 | tf_op jit(solution)/shard_map/ppermute | solution.py:32
  189.1 2.1 collective-permute-start.13
  191.3 2.2 collective-permute-start.3
  193.5 13.7 %collective-permute-start.4 = (bf16[2,1,104,512]{3,2,1,0:T(8,128)(2,1)S(1)}, bf16[2,1,104,512]{3,2,1,0:T(8,128)(2,1)S(1)}, u32[]{:S(2)}, u32[]{:S(2)}) collective-permute-start(bf16[2,1,104,512]{3,2,1,0:T(8,128)(2,1)S(1)} %get-tuple-element.31), channel_id=1, source_target_pairs={{1,0},{2,1},{3,2},{4,3},{5,4},{6,5},{7,6},{9,8},{10,9},{11,10},{12... | collective-permute-start | bytes 638984 | tf_op jit(solution)/shard_map/ppermute | solution.py:32
  208.0 12.1 %conv_two_own.1.refs_17_ = f32[2,4,104,512]{3,2,1,0:T(8,128)} custom-call(bf16[2,1,104,512]{3,2,1,0:T(8,128)(2,1)} %copy-done.7, bf16[2,4,104,512]{3,2,1,0:T(8,128)(2,1)} %get-tuple-element.21.refs_1_, bf16[2,1,104,512]{3,2,1,0:T(8,128)(2,1)} %copy-done.9, f32[128,128]{1,0:T(8,128)} %bitcast.34, f32[3]{0:T(128)} %add_convert_fusion.refs_2_.refs_4_, ...), custom_call_target="tpu_custom_call" | custom-call | flops 6341787648 | bytes 16000000 | tf_op jit(solution)/shard_map/conv_two_own/pallas_call | solution.py:224
  220.9 13.6 %conv_two_behind.1.block_ref = bf16[2,4,104,512]{3,2,1,0:T(8,128)(2,1)} custom-call(bf16[2,1,104,512]{3,2,1,0:T(8,128)(2,1)} %copy-done.6, bf16[2,4,104,512]{3,2,1,0:T(8,128)(2,1)} %copy-done.1, bf16[2,1,104,512]{3,2,1,0:T(8,128)(2,1)} %copy-done.8, f32[128,128]{1,0:T(8,128)} %bitcast.35, f32[3]{0:T(128)} %add_convert_fusion.refs_2_.refs_4_, ...), custom_call_target="tpu_custom_call" | custom-call | flops 6341787648 | bytes 16000000 | tf_op jit(solution)/shard_map/conv_two_behind/pallas_call | solution.py:224
  234.4 1.9 collective-permute-start.14
  236.4 22.1 %collective-permute-done.14.halo_ref = bf16[2,4,104,512]{3,2,1,0:T(8,128)(2,1)S(1)} collective-permute-done((bf16[2,4,104,512]{3,2,1,0:T(8,128)(2,1)}, bf16[2,4,104,512]{3,2,1,0:T(8,128)(2,1)S(1)}, u32[]{:S(2)}, u32[]{:S(2)}) %collective-permute-start.14) | collective-permute-done | bytes 852000 | tf_op jit(solution)/shard_map/ppermute | solution.py:32
  258.5 0.9 copy-done
  259.4 8.9 %upsample.1 = bf16[4,8,208,512]{3,2,1,0:T(8,128)(2,1)} custom-call(bf16[2,4,104,512]{3,2,1,0:T(8,128)(2,1)} %copy-done, bf16[2,4,104,512]{3,2,1,0:T(8,128)(2,1)} %conv_two_behind.1.block_ref, bf16[3,512,1024]{2,1,0:T(8,128)(2,1)} %w_ref.1, f32[1,1024]{1,0:T(1,128)} %bitcast.40), custom_call_target="tpu_custom_call" | custom-call | flops 3000000000 | bytes 12000000 | tf_op jit(solution)/shard_map/upsample/pallas_call | solution.py:272
  (57 shorter events, 8.3 us)
Async XLA Ops:
  6.5 28.0 %all-gather.9.cloned.1.call-start = ((), (), s32[]{:S(2)}) async-start(), calls=%async_computation.3 | async-start | bytes 1474560 | tf_op jit(solution)/shard_map/all_gather | solution.py:360
  8.3 88.4 %all-gather.13.cloned.1.call-start = ((), (), s32[]{:S(2)}) async-start(), calls=%async_computation.5 | async-start | bytes 9732096 | tf_op jit(solution)/shard_map/all_gather | solution.py:131
  34.6 23.3 %copy-start.5 = (bf16[12,3,2,16,512]{4,3,2,1,0:T(8,128)(2,1)S(1)}, bf16[12,3,2,16,512]{4,3,2,1,0:T(8,128)(2,1)}, u32[]{:S(2)}) copy-start(bf16[12,3,2,16,512]{4,3,2,1,0:T(8,128)(2,1)} %all-gather.9.cloned.1.call-done) | copy-start | bytes 3538948
  34.6 111.6 %all-gather.11.cloned.1.call-start = ((), (), s32[]{:S(2)}) async-start(), calls=%async_computation.4 | async-start | bytes 4866048 | tf_op jit(solution)/shard_map/all_gather | solution.py:131
  36.5 170.7 %all-gather.15.cloned.1.call-start = ((), (), s32[]{:S(2)}) async-start(), calls=%async_computation.6 | async-start | bytes 4866048 | tf_op jit(solution)/shard_map/all_gather | solution.py:131
  57.9 15.8 %copy-start.4 = (bf16[2,8,16,128]{3,2,1,0:T(8,128)(2,1)}, bf16[2,8,16,128]{3,2,1,0:T(8,128)(2,1)S(1)}, u32[]{:S(2)}) copy-start(bf16[2,8,16,128]{3,2,1,0:T(8,128)(2,1)S(1)} %reduce_sum.12.own_ref) | copy-start | bytes 196612
  57.9 34.5 %collective-permute-start.5 = (bf16[4,3,3,2,16,512]{5,4,3,2,1,0:T(8,128)(2,1)S(1)}, bf16[4,3,3,2,16,512]{5,4,3,2,1,0:T(8,128)(2,1)}, u32[]{:S(2)}, u32[]{:S(2)}) collective-permute-start(bf16[4,3,3,2,16,512]{5,4,3,2,1,0:T(8,128)(2,1)S(1)} %bitcast.47), channel_id=1, source_target_pairs={{0,32},{8,40},{16,48},{24,56},{32,64},{40,72},{48,80},{56,88},{64,... | collective-permute-start | bytes 3538952 | tf_op jit(solution)/shard_map/ppermute | solution.py:355
  59.4 34.4 %collective-permute-start.6 = (bf16[4,3,3,2,16,512]{5,4,3,2,1,0:T(8,128)(2,1)S(1)}, bf16[4,3,3,2,16,512]{5,4,3,2,1,0:T(8,128)(2,1)}, u32[]{:S(2)}, u32[]{:S(2)}) collective-permute-start(bf16[4,3,3,2,16,512]{5,4,3,2,1,0:T(8,128)(2,1)S(1)} %bitcast.48), channel_id=1, source_target_pairs={{0,96},{8,104},{16,112},{24,120},{32,0},{40,8},{48,16},{56,24},{64... | collective-permute-start | bytes 3538952 | tf_op jit(solution)/shard_map/ppermute | solution.py:355
  60.0 8.8 %collective-permute-start = (bf16[2,8,16,128]{3,2,1,0:T(8,128)(2,1)S(1)}, bf16[2,8,16,128]{3,2,1,0:T(8,128)(2,1)S(1)}, u32[]{:S(2)}, u32[]{:S(2)}) collective-permute-start(bf16[2,8,16,128]{3,2,1,0:T(8,128)(2,1)S(1)} %reduce_sum.12.own_ref), channel_id=1, source_target_pairs={{0,16},{8,24},{16,32},{24,40},{32,48},{40,56},{48,64},{56,72},{64,... | collective-permute-start | bytes 196616 | tf_op jit(solution)/shard_map/ppermute | solution.py:32
  65.3 8.4 %collective-permute-start.1 = (bf16[2,8,16,128]{3,2,1,0:T(8,128)(2,1)S(1)}, bf16[2,8,16,128]{3,2,1,0:T(8,128)(2,1)S(1)}, u32[]{:S(2)}, u32[]{:S(2)}) collective-permute-start(bf16[2,8,16,128]{3,2,1,0:T(8,128)(2,1)S(1)} %reduce_sum.12.own_ref), channel_id=1, source_target_pairs={{0,8},{8,16},{16,24},{24,32},{32,40},{40,48},{48,56},{56,64},{64,7... | collective-permute-start | bytes 196616 | tf_op jit(solution)/shard_map/ppermute | solution.py:32
  68.8 4.9 %copy-start.10 = (bf16[2,8,16,128]{3,2,1,0:T(8,128)(2,1)}, bf16[2,8,16,128]{3,2,1,0:T(8,128)(2,1)S(1)}, u32[]{:S(2)}) copy-start(bf16[2,8,16,128]{3,2,1,0:T(8,128)(2,1)S(1)} %collective-permute-done.early_ref) | copy-start | bytes 196612
  79.1 13.2 %all-to-all-start.1 = ((f32[128,1,128]{2,1,0:T(1,128)}), f32[128,1,128]{2,1,0:T(1,128)S(1)}, u32[]{:S(2)}, u32[]{:S(2)}) async-start(f32[128,1,128]{2,1,0:T(1,128)} %bitcast.39), calls=%async_computation.1 | async-start | bytes 131072 | tf_op jit(solution)/shard_map/all_to_all | solution.py:66
  92.3 4.4 %copy-start.3 = (f32[128,1,128]{2,1,0:T(1,128)}, f32[128,1,128]{2,1,0:T(1,128)S(1)}, u32[]{:S(2)}) copy-start(f32[128,1,128]{2,1,0:T(1,128)S(1)} %all-to-all-done.1) | copy-start | bytes 196612
  92.3 79.1 %collective-permute-start.8 = (bf16[4,3,3,2,16,512]{5,4,3,2,1,0:T(8,128)(2,1)S(1)}, bf16[4,3,3,2,16,512]{5,4,3,2,1,0:T(8,128)(2,1)}, u32[]{:S(2)}, u32[]{:S(2)}) collective-permute-start(bf16[4,3,3,2,16,512]{5,4,3,2,1,0:T(8,128)(2,1)S(1)} %bitcast.49), channel_id=1, source_target_pairs={{0,1},{1,0},{2,3},{3,2},{4,5},{5,4},{6,7},{7,6},{8,9},{9,8},{10,11... | collective-permute-start | bytes 3538952 | tf_op jit(solution)/shard_map/ppermute | solution.py:358
  92.3 65.8 %collective-permute-start.7 = (bf16[4,3,3,2,16,512]{5,4,3,2,1,0:T(8,128)(2,1)}, bf16[4,3,3,2,16,512]{5,4,3,2,1,0:T(8,128)(2,1)}, u32[]{:S(2)}, u32[]{:S(2)}) collective-permute-start(bf16[4,3,3,2,16,512]{5,4,3,2,1,0:T(8,128)(2,1)} %collective-permute-done.5.refs_10_), channel_id=1, source_target_pairs={{0,32},{8,40},{16,48},{24,56},{32,64},{40,72},{48,80},{56,88},{64,... | collective-permute-start | bytes 3538952 | tf_op jit(solution)/shard_map/ppermute | solution.py:355
  93.6 99.8 %collective-permute-start.9 = (bf16[4,3,3,2,16,512]{5,4,3,2,1,0:T(8,128)(2,1)}, bf16[4,3,3,2,16,512]{5,4,3,2,1,0:T(8,128)(2,1)}, u32[]{:S(2)}, u32[]{:S(2)}) collective-permute-start(bf16[4,3,3,2,16,512]{5,4,3,2,1,0:T(8,128)(2,1)} %collective-permute-done.5.refs_10_), channel_id=1, source_target_pairs={{0,1},{1,0},{2,3},{3,2},{4,5},{5,4},{6,7},{7,6},{8,9},{9,8},{10,11... | collective-permute-start | bytes 3538952 | tf_op jit(solution)/shard_map/ppermute | solution.py:358
  93.8 97.5 %collective-permute-start.10 = (bf16[4,3,3,2,16,512]{5,4,3,2,1,0:T(8,128)(2,1)}, bf16[4,3,3,2,16,512]{5,4,3,2,1,0:T(8,128)(2,1)}, u32[]{:S(2)}, u32[]{:S(2)}) collective-permute-start(bf16[4,3,3,2,16,512]{5,4,3,2,1,0:T(8,128)(2,1)} %collective-permute-done.6.refs_11_), channel_id=1, source_target_pairs={{0,1},{1,0},{2,3},{3,2},{4,5},{5,4},{6,7},{7,6},{8,9},{9,8},{10,11... | collective-permute-start | bytes 3538952 | tf_op jit(solution)/shard_map/ppermute | solution.py:358
  158.1 49.2 %collective-permute-start.11 = (bf16[4,3,3,2,16,512]{5,4,3,2,1,0:T(8,128)(2,1)}, bf16[4,3,3,2,16,512]{5,4,3,2,1,0:T(8,128)(2,1)}, u32[]{:S(2)}, u32[]{:S(2)}) collective-permute-start(bf16[4,3,3,2,16,512]{5,4,3,2,1,0:T(8,128)(2,1)} %collective-permute-done.7.refs_12_), channel_id=1, source_target_pairs={{0,1},{1,0},{2,3},{3,2},{4,5},{5,4},{6,7},{7,6},{8,9},{9,8},{10,11... | collective-permute-start | bytes 3538952 | tf_op jit(solution)/shard_map/ppermute | solution.py:358
  158.5 30.6 %collective-permute-start.2 = (bf16[2,4,104,512]{3,2,1,0:T(8,128)(2,1)}, bf16[2,4,104,512]{3,2,1,0:T(8,128)(2,1)S(1)}, u32[]{:S(2)}, u32[]{:S(2)}) collective-permute-start(bf16[2,4,104,512]{3,2,1,0:T(8,128)(2,1)} %get-tuple-element.21.refs_1_), channel_id=1, source_target_pairs={{0,8},{8,16},{16,24},{24,32},{32,40},{40,48},{48,56},{56,64},{64,7... | collective-permute-start | bytes 2555912 | tf_op jit(solution)/shard_map/ppermute | solution.py:32
  160.6 46.6 %all-to-all-start.2 = ((f32[128,1,128]{2,1,0:T(1,128)}), f32[128,1,128]{2,1,0:T(1,128)S(1)}, u32[]{:S(2)}, u32[]{:S(2)}) async-start(f32[128,1,128]{2,1,0:T(1,128)} %bitcast.36), calls=%async_computation.2 | async-start | bytes 131072 | tf_op jit(solution)/shard_map/all_to_all | solution.py:66
  171.5 35.8 %collective-permute-start.12 = (bf16[2,1,104,512]{3,2,1,0:T(8,128)(2,1)S(1)}, bf16[2,1,104,512]{3,2,1,0:T(8,128)(2,1)S(1)}, u32[]{:S(2)}, u32[]{:S(2)}) collective-permute-start(bf16[2,1,104,512]{3,2,1,0:T(8,128)(2,1)S(1)} %get-tuple-element.30), channel_id=1, source_target_pairs={{0,1},{1,2},{2,3},{3,4},{4,5},{5,6},{6,7},{8,9},{9,10},{10,11},{11... | collective-permute-start | bytes 638984 | tf_op jit(solution)/shard_map/ppermute | solution.py:32
  189.1 31.0 %copy-start.1 = (bf16[2,4,104,512]{3,2,1,0:T(8,128)(2,1)}, bf16[2,4,104,512]{3,2,1,0:T(8,128)(2,1)S(1)}, u32[]{:S(2)}) copy-start(bf16[2,4,104,512]{3,2,1,0:T(8,128)(2,1)S(1)} %collective-permute-done.2.refs_1_) | copy-start | bytes 2555908
  189.1 18.2 %collective-permute-start.13 = (bf16[2,1,104,512]{3,2,1,0:T(8,128)(2,1)S(1)}, bf16[2,1,104,512]{3,2,1,0:T(8,128)(2,1)S(1)}, u32[]{:S(2)}, u32[]{:S(2)}) collective-permute-start(bf16[2,1,104,512]{3,2,1,0:T(8,128)(2,1)S(1)} %get-tuple-element.29), channel_id=1, source_target_pairs={{1,0},{2,1},{3,2},{4,3},{5,4},{6,5},{7,6},{9,8},{10,9},{11,10},{12... | collective-permute-start | bytes 638984 | tf_op jit(solution)/shard_map/ppermute | solution.py:32
  191.3 28.8 %collective-permute-start.3 = (bf16[2,1,104,512]{3,2,1,0:T(8,128)(2,1)S(1)}, bf16[2,1,104,512]{3,2,1,0:T(8,128)(2,1)S(1)}, u32[]{:S(2)}, u32[]{:S(2)}) collective-permute-start(bf16[2,1,104,512]{3,2,1,0:T(8,128)(2,1)S(1)} %get-tuple-element.32), channel_id=1, source_target_pairs={{0,1},{1,2},{2,3},{3,4},{4,5},{5,6},{6,7},{8,9},{9,10},{10,11},{11... | collective-permute-start | bytes 638984 | tf_op jit(solution)/shard_map/ppermute | solution.py:32
  193.5 26.6 %collective-permute-start.4 = (bf16[2,1,104,512]{3,2,1,0:T(8,128)(2,1)S(1)}, bf16[2,1,104,512]{3,2,1,0:T(8,128)(2,1)S(1)}, u32[]{:S(2)}, u32[]{:S(2)}) collective-permute-start(bf16[2,1,104,512]{3,2,1,0:T(8,128)(2,1)S(1)} %get-tuple-element.31), channel_id=1, source_target_pairs={{1,0},{2,1},{3,2},{4,3},{5,4},{6,5},{7,6},{9,8},{10,9},{11,10},{12... | collective-permute-start | bytes 638984 | tf_op jit(solution)/shard_map/ppermute | solution.py:32
  207.2 0.6 copy-start.2
  207.2 0.7 copy-start.7
  207.3 0.7 copy-start.9
  220.1 0.7 copy-start.6
  220.1 0.7 copy-start.8
  234.4 24.0 %collective-permute-start.14 = (bf16[2,4,104,512]{3,2,1,0:T(8,128)(2,1)}, bf16[2,4,104,512]{3,2,1,0:T(8,128)(2,1)S(1)}, u32[]{:S(2)}, u32[]{:S(2)}) collective-permute-start(bf16[2,4,104,512]{3,2,1,0:T(8,128)(2,1)} %conv_two_behind.1.block_ref), channel_id=1, source_target_pairs={{0,8},{8,16},{16,24},{24,32},{32,40},{40,48},{48,56},{56,64},{64,7... | collective-permute-start | bytes 2555912 | tf_op jit(solution)/shard_map/ppermute | solution.py:32
  258.5 0.9 copy-start
  (1 other events, 0.6 us)
Sparse Core Ops, SparseCore 0:
  9.0 25.4 all-gather.8
  36.8 59.8 all-gather.12
  99.0 47.1 all-gather.10
  148.3 48.8 all-gather.14

commit v2 on v1

--- a/solution.py
+++ b/solution.py
@@ -106,43 +106,45 @@
     return lax.optimization_barrier((value, earlier))[0]
 
 
-def device_groups(inside, outside):
-    sizes = {"y": 4, "x": 4, "z": 4, "c": 2}
-
-    def walk(names, fixed):
-        if not names:
-            return [(fixed["y"] * 4 + fixed["x"]) * 8 + fixed["z"] * 2 + fixed["c"]]
-        return [k for i in range(sizes[names[0]]) for k in walk(names[1:], {**fixed, names[0]: i})]
-
-    def settings(names):
-        if not names:
-            return [{}]
-        return [{**rest, names[0]: i} for i in range(sizes[names[0]]) for rest in settings(names[1:])]
-
-    return [walk(inside, fixed) for fixed in settings(outside)]
-
-
 def quarter_of(weight, low, high, pos):
     taps = jnp.swapaxes(weight, 3, 4)
     return lax.dynamic_slice(taps, (0, 0, low, 16 * pos, 0), (3, 3, high - low, 16, CH))
 
 
-def gather_plane(quarter):
-    return lax.all_gather(quarter, ("frame", "height"), axis_index_groups=device_groups("zxc", "y"))
-
-
-def plane_plan(array, low, high):
-    return [
-        (array, 8 * z + 2 * x + c, e - low, e, ("fixed", 2 * z + c, x))
-        for e in range(low, high)
-        for z in range(4)
-        for x in range(4)
-        for c in range(2)
-    ]
+def stack_kernel(*refs):
+    *parts, out_ref, sems = refs
+    copies = [pltpu.make_async_copy(part, out_ref.at[k], sems.at[k]) for k, part in enumerate(parts)]
+    for copy in copies:
+        copy.start()
+    for copy in copies:
+        copy.wait()
+
+
+def stack(parts):
+    return pl.pallas_call(
+        stack_kernel,
+        in_specs=[ANY] * len(parts),
+        out_specs=ANY,
+        out_shape=jax.ShapeDtypeStruct((len(parts), *parts[0].shape), parts[0].dtype),
+        scratch_shapes=[pltpu.SemaphoreType.DMA((len(parts),))],
+        cost_estimate=pl.CostEstimate(flops=0, bytes_accessed=4 * 10**6, transcendentals=0),
+        name="stack_parts",
+    )(*parts)
+
+
+def gather_columns(weight, low, high):
+    return lax.all_gather(jnp.swapaxes(weight[:, :, low:high], 3, 4), "height", axis=3, tiled=True)
+
+
+def whole_plan(array, low, high):
+    return [(array, None, e - low, e, ("whole", 0, 0)) for e in range(low, high)]
+
+
+Z_SHIFTS = (0, 3, 1, 2)
 
 
 def ring_plan(array, low, high, flip, step):
-    return [(array, z, e - low, e, (flip, z, step)) for e in range(low, high) for z in range(4)]
+    return [(array, k, e - low, e, (flip, z, step)) for e in range(low, high) for k, z in enumerate(Z_SHIFTS)]
 
 
 def conv_kernel(pieces, products, taps, plan, weights, extras, *refs):
@@ -157,15 +159,18 @@
     stat_ref = refs.pop(0) if "stat" in extras else None
     field, wbuf, acc, sems = refs
     low, high = taps[0], taps[-1] + 1
-    core, ring = place_ref[0], place_ref[1]
+    core, ring, z = place_ref[0], place_ref[1], place_ref[2]
     columns = sorted({copy[3] for copy in plan})
-    for array, index, source_e, e, (kind, block, quarter) in plan:
-        if kind != "fixed":
-            block = 2 * block + (1 - core if kind == "other" else core)
-            quarter = lax.rem(ring + quarter, 4)
-        rows = pl.multiple_of(block * 64 + quarter * 16, 16)
-        source = w_refs[array].at[index, pl.ds(low, high - low), :, source_e]
-        pltpu.make_async_copy(source, wbuf.at[columns.index(e), :, :, pl.ds(rows, 16)], sems.at[columns.index(e)]).start()
+    for array, index, source_e, e, (kind, shift, step) in plan:
+        slot = columns.index(e)
+        if kind == "whole":
+            source, target = w_refs[array].at[pl.ds(low, high - low), :, source_e], wbuf.at[slot]
+        else:
+            block = 2 * lax.rem(z + shift, 4) + (1 - core if kind == "other" else core)
+            rows = pl.multiple_of(block * 64 + lax.rem(ring + step, 4) * 16, 16)
+            source = w_refs[array].at[index, pl.ds(low, high - low), :, source_e]
+            target = wbuf.at[slot, :, :, pl.ds(rows, 16)]
+        pltpu.make_async_copy(source, target, sems.at[slot]).start()
     mean, inverse = combine_stats(stats_ref, CELLS * (CH // GROUPS))
     scale = inverse * gain_ref[...]
     offset = offset_ref[...]
@@ -346,8 +351,8 @@
 ):
     devices = lax.axis_size("frame") * lax.axis_size("height")
     slab, tile = lax.axis_index("frame"), lax.axis_index("height")
-    in_x, in_y = slab % 4, slab // 4
-    place = jnp.stack([tile % 2, in_y]).astype(jnp.int32)
+    in_y = slab // 4
+    place = jnp.stack([tile % 2, in_y, tile // 2]).astype(jnp.int32)
     flags = jnp.stack([slab > 0, tile > 0, tile < lax.axis_size("height") - 1]).astype(F32)
     row = lambda v: v.reshape(1, -1)
 
@@ -357,19 +362,20 @@
     def swap_core(v):
         return lax.ppermute(v, "height", [(i, i ^ 1) for i in range(8)])
 
-    near = lax.all_gather(
-        quarter_of(weight_two, 1, 3, in_y), ("frame", "height"), axis_index_groups=device_groups("z", "yxc")
-    )
-    one_a = gather_plane(after(quarter_of(weight_one, 0, 2, in_x), near))
-    one_b = gather_plane(after(quarter_of(weight_one, 2, 3, in_x), near))
-    two_a = gather_plane(after(quarter_of(weight_two, 0, 1, in_x), near))
-
+    def send_z(v, k):
+        return lax.ppermute(v, "height", [(i, (i + 2 * k) % 8) for i in range(8)])
+
+    quarter = quarter_of(weight_two, 1, 3, in_y)
+    sent = [quarter, *[send_z(quarter, k) for k in (1, 3, 2)]]
+    one = gather_columns(weight_one, 0, 3)
     latent = latent_field(tokens, token_pos)
-    near = after(near, latent[2])
+    two = gather_columns(after(weight_two, latent[2]), 0, 1)
+    near = stack([after(v, latent[2]) for v in sent])
     left, right = send_y(near, 1), send_y(near, -1)
     base, stat = input_conv(latent, weight_in.reshape(-1, CH), row(bias_in), devices)
     shared = share_stats(stat)
     far = send_y(after(left, shared), 1)
+    swapped = [swap_core(after(v, shared)) for v in (near, left, right)]
 
     def edges(j):
         return [1] if j == 0 else [2] if j == RH + 1 else []
@@ -377,24 +383,20 @@
     everything = lambda i, j: ([0] if i < FT else []) + edges(j)
     norm_one = (shared, flags, place, row(gain_one), row(offset_one))
     common = ([base], [(0, 2 * FT, 0, RH + 2, everything)], [(t, t + a, a) for t in range(FT) for a in range(3)])
-    (partial,) = block_conv(
-        "conv_one_first", *common, *norm_one, ([one_a], plane_plan(0, 0, 2)), {}, F32, devices
-    )
-    swapped = [swap_core(after(v, shared)) for v in (near, left, right)]
     inner, stat = block_conv(
-        "conv_one_last",
+        "conv_one",
         *common,
         *norm_one,
-        ([one_b], plane_plan(0, 2, 3)),
-        {"partial": partial, "bias": row(bias_one), "stat": None},
+        ([one], whole_plan(0, 0, 3)),
+        {"bias": row(bias_one), "stat": None},
         BF16,
         devices,
     )
     shared = share_stats(stat)
-    behind = along(inner, "frame", 1)
+    behind = along(after(inner, shared), "frame", 1)
     swapped.append(swap_core(after(far, inner)))
-    arrays = [two_a, near, left, right, far, *swapped]
-    plan = plane_plan(0, 0, 1)
+    arrays = [two, near, left, right, far, *swapped]
+    plan = whole_plan(0, 0, 1)
     for k, step in enumerate((0, 3, 1, 2)):
         plan += ring_plan(1 + k, 1, 3, "own", step) + ring_plan(5 + k, 1, 3, "other", step)
     kernel_two = (arrays, plan)
@@ -421,7 +423,7 @@
     )
     (block,) = block_conv(
         "conv_two_behind",
-        rows_around(behind),
+        rows_around(after(behind, partial)),
         pieces([0]),
         [(0, 0, 0), (0, 1, 1), (1, 1, 0)],
         *norm_two,

time: 278 us -> 269 us (0.968)
  waiting for transfers between devices: 111 us -> 75.6 us
  Pallas kernels: 69 us -> 99.1 us
  blocking collectives: 16.5 us -> 30.6 us
  starting transfers between devices: 51.8 us -> 39.6 us
  local copies, waits for them, and re-layouts: 10.6 us -> 6.85 us
    all_gather x4 -> x2, waiting for transfers between devices: 60.8 us -> 0.02 us  [gather_columns(): lax.all_gather(jnp.swapaxes(weight[:, :, low:high], 3, 4), 'height', axis...]
    pallas_call x0 -> x1, Pallas kernels: none -> 36.9 us  [stack(): pl.pallas_call(stack_kernel, in_specs=[ANY] * len(parts), out_specs=ANY,...]
    ppermute x0 -> x3, waiting for transfers between devices: none -> 26 us  [send_z(): return lax.ppermute(v, 'height', [(i, (i + 2 * k) % 8) for i in range(8)])]
    all_to_all x0 -> x1, blocking collectives: none -> 16.2 us  [share_stats(): return lax.all_to_all(stat, ('frame', 'height'), 0, 0, tiled=True)]
    all_to_all x2 -> x1, starting transfers between devices: 15.3 us -> 6.45 us  [share_stats(): return lax.all_to_all(stat, ('frame', 'height'), 0, 0, tiled=True)]
    ppermute x8, waiting for transfers between devices: 42.9 us -> 34.4 us  [along(): lax.ppermute(value, axis, [(source, source + steps) for source in range(l...]
    ppermute x3, waiting for transfers between devices: 0.01 us -> 7.4 us  [send_y(): lax.ppermute(v, 'frame', [(4 * y + x, 4 * ((y + k) % 4) + x) for y in ran...]
    pallas_call x4 -> x3, Pallas kernels: 53 us -> 46.1 us  [block_conv(): pl.pallas_call(functools.partial(conv_kernel, pieces, products, taps, pla...]
  transfers between devices with their start and end apart: 21 -> 21, of which waited for: 8 -> 11; matrix products, arithmetic and copies ran while one was open for 3% -> 2% of each run, Pallas kernels for 17% -> 29%
where the time goes in v2:
time: 269 us; the launch traced here: 268 us
  Pallas kernels  99.1 us (37%)
  waiting for transfers between devices  75.6 us (28%)
  starting transfers between devices  39.6 us (15%)
  blocking collectives  30.6 us (11%)
  between operations  13.7 us (5%)
  local copies, waits for them, and re-layouts  6.85 us (3%)
    pallas_call x3, Pallas kernels, block_conv(): pl.pallas_call(functools.partial(conv_kernel, pieces, products, taps, pla...  46.1 us
    pallas_call x1, Pallas kernels, stack(): pl.pallas_call(stack_kernel, in_specs=[ANY] * len(parts), out_specs=ANY,...  36.9 us
    ppermute x8, waiting for transfers between devices, along(): lax.ppermute(value, axis, [(source, source + steps) for source in range(l...  34.4 us
    ppermute x3, waiting for transfers between devices, send_z(): return lax.ppermute(v, 'height', [(i, (i + 2 * k) % 8) for i in range(8)])  26 us
    ppermute x8, starting transfers between devices, along(): lax.ppermute(value, axis, [(source, source + steps) for source in range(l...  24.9 us
    all_to_all x1, blocking collectives, share_stats(): return lax.all_to_all(stat, ('frame', 'height'), 0, 0, tiled=True)  16.2 us
    all_to_all x1, blocking collectives, latent_field(): grids = lax.all_to_all(grids, 'height', 0, 0, tiled=True)  14.4 us
    pallas_call x1, Pallas kernels, upsample(): pl.pallas_call(upsample_kernel, grid=(FT, 2), in_specs=[pl.BlockSpec((FT,...  8.94 us
  transfers between devices with their start and end apart: 21, of which 11 were waited for; matrix products, arithmetic and copies ran while one was open for 2% of the time, Pallas kernels for 29%

profile of v2, /device:TPU:40, one launch (start us, length us, event | category | flops | bytes accessed | tf_op | source)
XLA Modules:
  0.0 267.6 jit_solution(3862716915378458905)
XLA Ops:
  9.4 2.2 place_tokens.1
  11.6 14.4 %all_to_all.27 = bf16[8,2,8,16,128]{4,3,2,1,0:T(8,128)(2,1)S(1)} all-to-all(bf16[8,2,8,16,128]{4,3,2,1,0:T(8,128)(2,1)} %place_tokens.1), channel_id=1, replica_groups=mesh['frame'=16,'height'=8] {'height'}, dimensions={0} | all-to-all | bytes 1048576 | tf_op jit(solution)/shard_map/all_to_all | solution.py:331
  27.4 2.1 collective-permute-start.6
  29.5 2.0 collective-permute-start.7
  31.5 12.1 %collective-permute-done.5.refs_1_ = bf16[3,3,2,16,512]{4,3,2,1,0:T(8,128)(2,1)S(1)} collective-permute-done((bf16[3,3,2,16,512]{4,3,2,1,0:T(8,128)(2,1)S(1)}, bf16[3,3,2,16,512]{4,3,2,1,0:T(8,128)(2,1)S(1)}, u32[]{:S(2)}, u32[]{:S(2)}) %collective-permute-start.5) | collective-permute-done | bytes 294944 | tf_op jit(solution)/shard_map/ppermute | solution.py:366
  43.6 13.9 %collective-permute-done.7.refs_3_ = bf16[3,3,2,16,512]{4,3,2,1,0:T(8,128)(2,1)S(1)} collective-permute-done((bf16[3,3,2,16,512]{4,3,2,1,0:T(8,128)(2,1)S(1)}, bf16[3,3,2,16,512]{4,3,2,1,0:T(8,128)(2,1)S(1)}, u32[]{:S(2)}, u32[]{:S(2)}) %collective-permute-start.7) | collective-permute-done | bytes 294944 | tf_op jit(solution)/shard_map/ppermute | solution.py:366
  58.3 36.9 %stack_parts.1.refs_9_ = bf16[4,3,3,2,16,512]{5,4,3,2,1,0:T(8,128)(2,1)} custom-call(bf16[3,3,2,16,512]{4,3,2,1,0:T(8,128)(2,1)} %copy-done, bf16[3,3,2,16,512]{4,3,2,1,0:T(8,128)(2,1)} %copy-done.4, bf16[3,3,2,16,512]{4,3,2,1,0:T(8,128)(2,1)} %copy-done.5, bf16[3,3,2,16,512]{4,3,2,1,0:T(8,128)(2,1)} %copy-done.6), custom_call_target="tpu_custom_call" | custom-call | bytes 4000000 | tf_op jit(solution)/shard_map/stack_parts/pallas_call | solution.py:124
  95.2 1.8 collective-permute-start.8
  97.3 4.9 %collective-permute-start = (bf16[2,8,16,128]{3,2,1,0:T(8,128)(2,1)S(1)}, bf16[2,8,16,128]{3,2,1,0:T(8,128)(2,1)S(1)}, u32[]{:S(2)}, u32[]{:S(2)}) collective-permute-start(bf16[2,8,16,128]{3,2,1,0:T(8,128)(2,1)S(1)} %reduce_sum.12.own_ref), channel_id=1, source_target_pairs={{0,16},{8,24},{16,32},{24,40},{32,48},{40,56},{48,64},{56,72},{64,... | collective-permute-start | bytes 196616 | tf_op jit(solution)/shard_map/ppermute | solution.py:32
  102.2 2.5 collective-permute-start.1
  106.5 4.1 %collective-permute-done.1.behind_ref = bf16[2,8,16,128]{3,2,1,0:T(8,128)(2,1)S(1)} collective-permute-done((bf16[2,8,16,128]{3,2,1,0:T(8,128)(2,1)S(1)}, bf16[2,8,16,128]{3,2,1,0:T(8,128)(2,1)S(1)}, u32[]{:S(2)}, u32[]{:S(2)}) %collective-permute-start.1) | collective-permute-done | bytes 65568 | tf_op jit(solution)/shard_map/ppermute | solution.py:32
  111.2 5.0 %input_conv.1 = (bf16[4,6,104,512]{3,2,1,0:T(8,128)(2,1)}, f32[128,128]{1,0:T(8,128)}) custom-call(bf16[2,8,16,128]{3,2,1,0:T(8,128)(2,1)} %copy-done.14, bf16[2,8,16,128]{3,2,1,0:T(8,128)(2,1)} %copy-done.15, bf16[2,8,16,128]{3,2,1,0:T(8,128)(2,1)} %copy-done.9, bf16[432,512]{1,0:T(8,128)(2,1)} %bitcast.35, f32[1,512]{1,0:T(1,128)} %bitcast.36), custom_call_target="tpu_custom_call" | custom-call | flops 3000000000 | bytes 4000000 | tf_op jit(solution)/shard_map/input_conv/pallas_call | solution.py:91
  116.2 6.5 %all-to-all-start.1 = ((f32[128,1,128]{2,1,0:T(1,128)}), f32[128,1,128]{2,1,0:T(1,128)S(1)}, u32[]{:S(2)}, u32[]{:S(2)}) async-start(f32[128,1,128]{2,1,0:T(1,128)} %bitcast.32), calls=%async_computation.1 | async-start | bytes 131072 | tf_op jit(solution)/shard_map/all_to_all | solution.py:66
  123.3 7.0 %all-to-all-done.1 = f32[128,1,128]{2,1,0:T(1,128)S(1)} async-done(((f32[128,1,128]{2,1,0:T(1,128)}), f32[128,1,128]{2,1,0:T(1,128)S(1)}, u32[]{:S(2)}, u32[]{:S(2)}) %all-to-all-start.1) | async-done | bytes 65568 | tf_op jit(solution)/shard_map/all_to_all | solution.py:66
  131.8 19.8 %conv_one.1 = (bf16[2,4,104,512]{3,2,1,0:T(8,128)(2,1)}, f32[128,128]{1,0:T(8,128)}) custom-call(bf16[4,6,104,512]{3,2,1,0:T(8,128)(2,1)} %get-tuple-element.20.refs_0_.refs_19_, f32[128,128]{1,0:T(8,128)} %bitcast.31, f32[3]{0:T(128)} %add_convert_fusion.refs_2_.refs_4_, s32[3]{0:T(128)} %pad_add_fusion.refs_3_.refs_5_, f32[1,512]{1,0:T(1,128)} %bitcast.37, ...), custom_call_target="tpu_custom_call" | custom-call | flops 12683575296 | bytes 16000000 | tf_op jit(solution)/shard_map/conv_one/pallas_call | solution.py:229
  151.6 7.4 %collective-permute-done.10.refs_12_ = bf16[4,3,3,2,16,512]{5,4,3,2,1,0:T(8,128)(2,1)} collective-permute-done((bf16[4,3,3,2,16,512]{5,4,3,2,1,0:T(8,128)(2,1)}, bf16[4,3,3,2,16,512]{5,4,3,2,1,0:T(8,128)(2,1)}, u32[]{:S(2)}, u32[]{:S(2)}) %collective-permute-start.10) | collective-permute-done | bytes 1179680 | tf_op jit(solution)/shard_map/ppermute | solution.py:360
  159.0 16.2 %all_to_all.28 = f32[128,1,128]{2,1,0:T(1,128)} all-to-all(f32[128,1,128]{2,1,0:T(1,128)} %bitcast.33), channel_id=1, replica_groups=mesh['frame'=16,'height'=8] {'frame','height'}, dimensions={0} | all-to-all | bytes 131072 | tf_op jit(solution)/shard_map/all_to_all | solution.py:66
  175.2 2.6 collective-permute-start.2
  177.8 1.1 fusion.4
  178.9 1.9 collective-permute-start.3
  180.9 3.6 %collective-permute-start.4 = (bf16[2,1,104,512]{3,2,1,0:T(8,128)(2,1)S(1)}, bf16[2,1,104,512]{3,2,1,0:T(8,128)(2,1)S(1)}, u32[]{:S(2)}, u32[]{:S(2)}) collective-permute-start(bf16[2,1,104,512]{3,2,1,0:T(8,128)(2,1)S(1)} %get-tuple-element.37), channel_id=1, source_target_pairs={{1,0},{2,1},{3,2},{4,3},{5,4},{6,5},{7,6},{9,8},{10,9},{11,10},{12... | collective-permute-start | bytes 638984 | tf_op jit(solution)/shard_map/ppermute | solution.py:32
  184.6 1.5 collective-permute-done.3.refs_0_
  186.1 1.8 collective-permute-done.4.refs_2_
  188.5 12.5 %conv_two_own.1.refs_17_ = f32[2,4,104,512]{3,2,1,0:T(8,128)} custom-call(bf16[2,1,104,512]{3,2,1,0:T(8,128)(2,1)} %copy-done.11, bf16[2,4,104,512]{3,2,1,0:T(8,128)(2,1)} %get-tuple-element.24.refs_1_, bf16[2,1,104,512]{3,2,1,0:T(8,128)(2,1)} %copy-done.13, f32[128,128]{1,0:T(8,128)} %bitcast.29, f32[3]{0:T(128)} %add_convert_fusion.refs_2_.refs_4_, ...), custom_call_target="tpu_custom_call" | custom-call | flops 6341787648 | bytes 16000000 | tf_op jit(solution)/shard_map/conv_two_own/pallas_call | solution.py:229
  201.1 3.3 %collective-permute-start.15 = (bf16[2,1,104,512]{3,2,1,0:T(8,128)(2,1)S(1)}, bf16[2,1,104,512]{3,2,1,0:T(8,128)(2,1)S(1)}, u32[]{:S(2)}, u32[]{:S(2)}) collective-permute-start(bf16[2,1,104,512]{3,2,1,0:T(8,128)(2,1)S(1)} %get-tuple-element.36), channel_id=1, source_target_pairs={{0,1},{1,2},{2,3},{3,4},{4,5},{5,6},{6,7},{8,9},{9,10},{10,11},{11... | collective-permute-start | bytes 638984 | tf_op jit(solution)/shard_map/ppermute | solution.py:32
  204.5 3.0 %collective-permute-start.16 = (bf16[2,1,104,512]{3,2,1,0:T(8,128)(2,1)S(1)}, bf16[2,1,104,512]{3,2,1,0:T(8,128)(2,1)S(1)}, u32[]{:S(2)}, u32[]{:S(2)}) collective-permute-start(bf16[2,1,104,512]{3,2,1,0:T(8,128)(2,1)S(1)} %get-tuple-element.35), channel_id=1, source_target_pairs={{1,0},{2,1},{3,2},{4,3},{5,4},{6,5},{7,6},{9,8},{10,9},{11,10},{12... | collective-permute-start | bytes 638984 | tf_op jit(solution)/shard_map/ppermute | solution.py:32
  207.4 1.3 collective-permute-done.15.refs_0_
  208.8 1.8 collective-permute-done.16.refs_2_
  211.2 13.8 %conv_two_behind.1.block_ref = bf16[2,4,104,512]{3,2,1,0:T(8,128)(2,1)} custom-call(bf16[2,1,104,512]{3,2,1,0:T(8,128)(2,1)} %copy-done.10, bf16[2,4,104,512]{3,2,1,0:T(8,128)(2,1)} %copy-done.7, bf16[2,1,104,512]{3,2,1,0:T(8,128)(2,1)} %copy-done.12, f32[128,128]{1,0:T(8,128)} %bitcast.30, f32[3]{0:T(128)} %add_convert_fusion.refs_2_.refs_4_, ...), custom_call_target="tpu_custom_call" | custom-call | flops 6341787648 | bytes 16000000 | tf_op jit(solution)/shard_map/conv_two_behind/pallas_call | solution.py:229
  225.1 3.0 %collective-permute-start.17 = (bf16[2,4,104,512]{3,2,1,0:T(8,128)(2,1)}, bf16[2,4,104,512]{3,2,1,0:T(8,128)(2,1)S(1)}, u32[]{:S(2)}, u32[]{:S(2)}) collective-permute-start(bf16[2,4,104,512]{3,2,1,0:T(8,128)(2,1)} %conv_two_behind.1.block_ref), channel_id=1, source_target_pairs={{0,8},{8,16},{16,24},{24,32},{32,40},{40,48},{48,56},{56,64},{64,7... | collective-permute-start | bytes 2555912 | tf_op jit(solution)/shard_map/ppermute | solution.py:32
  228.1 22.9 %collective-permute-done.17.halo_ref = bf16[2,4,104,512]{3,2,1,0:T(8,128)(2,1)S(1)} collective-permute-done((bf16[2,4,104,512]{3,2,1,0:T(8,128)(2,1)}, bf16[2,4,104,512]{3,2,1,0:T(8,128)(2,1)S(1)}, u32[]{:S(2)}, u32[]{:S(2)}) %collective-permute-start.17) | collective-permute-done | bytes 852000 | tf_op jit(solution)/shard_map/ppermute | solution.py:32
  251.9 8.9 %upsample.1 = bf16[4,8,208,512]{3,2,1,0:T(8,128)(2,1)} custom-call(bf16[2,4,104,512]{3,2,1,0:T(8,128)(2,1)} %copy-done.2, bf16[2,4,104,512]{3,2,1,0:T(8,128)(2,1)} %conv_two_behind.1.block_ref, bf16[3,512,1024]{2,1,0:T(8,128)(2,1)} %w_ref.1, f32[1,1024]{1,0:T(1,128)} %bitcast.34), custom_call_target="tpu_custom_call" | custom-call | flops 3000000000 | bytes 12000000 | tf_op jit(solution)/shard_map/upsample/pallas_call | solution.py:277
  (63 shorter events, 12.2 us)
Async XLA Ops:
  6.5 125.3 %all-gather.3.cloned.1.call-start = ((), (), s32[]{:S(2)}) async-start(), calls=%async_computation.3 | async-start | bytes 15925248 | tf_op jit(solution)/shard_map/all_gather | solution.py:136
  7.3 18.8 %copy-start.3 = (bf16[3,3,3,512,64]{3,4,2,1,0:T(8,128)(2,1)S(1)}, bf16[3,3,3,512,64]{3,4,2,1,0:T(8,128)(2,1)}, u32[]{:S(2)}) copy-start(bf16[3,3,3,512,64]{3,4,2,1,0:T(8,128)(2,1)} %param.24) | copy-start | bytes 5308420
  7.3 177.3 %all-gather.5.cloned.1.call-start = ((), (), s32[]{:S(2)}) async-start(), calls=%async_computation.4 | async-start | bytes 5308416 | tf_op jit(solution)/shard_map/all_gather | solution.py:136
  26.1 76.1 %copy-start.9 = (bf16[2,8,16,128]{3,2,1,0:T(8,128)(2,1)}, bf16[2,8,16,128]{3,2,1,0:T(8,128)(2,1)S(1)}, u32[]{:S(2)}) copy-start(bf16[2,8,16,128]{3,2,1,0:T(8,128)(2,1)S(1)} %reduce_sum.12.own_ref) | copy-start | bytes 196612
  27.0 30.5 %copy-start = (bf16[3,3,2,16,512]{4,3,2,1,0:T(8,128)(2,1)}, bf16[3,3,2,16,512]{4,3,2,1,0:T(8,128)(2,1)S(1)}, u32[]{:S(2)}) copy-start(bf16[3,3,2,16,512]{4,3,2,1,0:T(8,128)(2,1)S(1)} %dynamic-slice_bitcast_fusion.refs_0_) | copy-start | bytes 884740
  27.0 16.6 %collective-permute-start.5 = (bf16[3,3,2,16,512]{4,3,2,1,0:T(8,128)(2,1)S(1)}, bf16[3,3,2,16,512]{4,3,2,1,0:T(8,128)(2,1)S(1)}, u32[]{:S(2)}, u32[]{:S(2)}) collective-permute-start(bf16[3,3,2,16,512]{4,3,2,1,0:T(8,128)(2,1)S(1)} %dynamic-slice_bitcast_fusion.refs_0_), channel_id=1, source_target_pairs={{0,2},{1,3},{2,4},{3,5},{4,6},{5,7},{6,0},{7,1},{8,10},{9,11},{10,... | collective-permute-start | bytes 884744 | tf_op jit(solution)/shard_map/ppermute | solution.py:366
  27.4 16.2 %collective-permute-start.6 = (bf16[3,3,2,16,512]{4,3,2,1,0:T(8,128)(2,1)S(1)}, bf16[3,3,2,16,512]{4,3,2,1,0:T(8,128)(2,1)S(1)}, u32[]{:S(2)}, u32[]{:S(2)}) collective-permute-start(bf16[3,3,2,16,512]{4,3,2,1,0:T(8,128)(2,1)S(1)} %dynamic-slice_bitcast_fusion.refs_0_), channel_id=1, source_target_pairs={{0,6},{1,7},{2,0},{3,1},{4,2},{5,3},{6,4},{7,5},{8,14},{9,15},{10,... | collective-permute-start | bytes 884744 | tf_op jit(solution)/shard_map/ppermute | solution.py:366
  29.5 28.0 %collective-permute-start.7 = (bf16[3,3,2,16,512]{4,3,2,1,0:T(8,128)(2,1)S(1)}, bf16[3,3,2,16,512]{4,3,2,1,0:T(8,128)(2,1)S(1)}, u32[]{:S(2)}, u32[]{:S(2)}) collective-permute-start(bf16[3,3,2,16,512]{4,3,2,1,0:T(8,128)(2,1)S(1)} %dynamic-slice_bitcast_fusion.refs_0_), channel_id=1, source_target_pairs={{0,4},{1,5},{2,6},{3,7},{4,0},{5,1},{6,2},{7,3},{8,12},{9,13},{10,... | collective-permute-start | bytes 884744 | tf_op jit(solution)/shard_map/ppermute | solution.py:366
  43.6 13.9 %copy-start.4 = (bf16[3,3,2,16,512]{4,3,2,1,0:T(8,128)(2,1)}, bf16[3,3,2,16,512]{4,3,2,1,0:T(8,128)(2,1)S(1)}, u32[]{:S(2)}) copy-start(bf16[3,3,2,16,512]{4,3,2,1,0:T(8,128)(2,1)S(1)} %collective-permute-done.5.refs_1_) | copy-start | bytes 884740
  43.6 13.9 %copy-start.5 = (bf16[3,3,2,16,512]{4,3,2,1,0:T(8,128)(2,1)}, bf16[3,3,2,16,512]{4,3,2,1,0:T(8,128)(2,1)S(1)}, u32[]{:S(2)}) copy-start(bf16[3,3,2,16,512]{4,3,2,1,0:T(8,128)(2,1)S(1)} %collective-permute-done.6.refs_2_) | copy-start | bytes 884740
  95.2 35.1 %collective-permute-start.8 = (bf16[4,3,3,2,16,512]{5,4,3,2,1,0:T(8,128)(2,1)}, bf16[4,3,3,2,16,512]{5,4,3,2,1,0:T(8,128)(2,1)}, u32[]{:S(2)}, u32[]{:S(2)}) collective-permute-start(bf16[4,3,3,2,16,512]{5,4,3,2,1,0:T(8,128)(2,1)} %stack_parts.1.refs_9_), channel_id=1, source_target_pairs={{0,32},{8,40},{16,48},{24,56},{32,64},{40,72},{48,80},{56,88},{64,... | collective-permute-start | bytes 3538952 | tf_op jit(solution)/shard_map/ppermute | solution.py:360
  96.9 34.6 %collective-permute-start.9 = (bf16[4,3,3,2,16,512]{5,4,3,2,1,0:T(8,128)(2,1)}, bf16[4,3,3,2,16,512]{5,4,3,2,1,0:T(8,128)(2,1)}, u32[]{:S(2)}, u32[]{:S(2)}) collective-permute-start(bf16[4,3,3,2,16,512]{5,4,3,2,1,0:T(8,128)(2,1)} %stack_parts.1.refs_9_), channel_id=1, source_target_pairs={{0,96},{8,104},{16,112},{24,120},{32,0},{40,8},{48,16},{56,24},{64... | collective-permute-start | bytes 3538952 | tf_op jit(solution)/shard_map/ppermute | solution.py:360
  97.3 9.2 %collective-permute-start = (bf16[2,8,16,128]{3,2,1,0:T(8,128)(2,1)S(1)}, bf16[2,8,16,128]{3,2,1,0:T(8,128)(2,1)S(1)}, u32[]{:S(2)}, u32[]{:S(2)}) collective-permute-start(bf16[2,8,16,128]{3,2,1,0:T(8,128)(2,1)S(1)} %reduce_sum.12.own_ref), channel_id=1, source_target_pairs={{0,16},{8,24},{16,32},{24,40},{32,48},{40,56},{48,64},{56,72},{64,... | collective-permute-start | bytes 196616 | tf_op jit(solution)/shard_map/ppermute | solution.py:32
  102.2 8.4 %collective-permute-start.1 = (bf16[2,8,16,128]{3,2,1,0:T(8,128)(2,1)S(1)}, bf16[2,8,16,128]{3,2,1,0:T(8,128)(2,1)S(1)}, u32[]{:S(2)}, u32[]{:S(2)}) collective-permute-start(bf16[2,8,16,128]{3,2,1,0:T(8,128)(2,1)S(1)} %reduce_sum.12.own_ref), channel_id=1, source_target_pairs={{0,8},{8,16},{16,24},{24,32},{32,40},{40,48},{48,56},{56,64},{64,7... | collective-permute-start | bytes 196616 | tf_op jit(solution)/shard_map/ppermute | solution.py:32
  106.5 4.1 %copy-start.14 = (bf16[2,8,16,128]{3,2,1,0:T(8,128)(2,1)}, bf16[2,8,16,128]{3,2,1,0:T(8,128)(2,1)S(1)}, u32[]{:S(2)}) copy-start(bf16[2,8,16,128]{3,2,1,0:T(8,128)(2,1)S(1)} %collective-permute-done.early_ref) | copy-start | bytes 196612
  111.2 19.1 %copy-start.1 = (bf16[4,3,3,2,16,512]{5,4,3,2,1,0:T(8,128)(2,1)S(1)}, bf16[4,3,3,2,16,512]{5,4,3,2,1,0:T(8,128)(2,1)}, u32[]{:S(2)}) copy-start(bf16[4,3,3,2,16,512]{5,4,3,2,1,0:T(8,128)(2,1)} %stack_parts.1.refs_9_) | copy-start | bytes 3538948
  116.2 14.1 %all-to-all-start.1 = ((f32[128,1,128]{2,1,0:T(1,128)}), f32[128,1,128]{2,1,0:T(1,128)S(1)}, u32[]{:S(2)}, u32[]{:S(2)}) async-start(f32[128,1,128]{2,1,0:T(1,128)} %bitcast.32), calls=%async_computation.1 | async-start | bytes 131072 | tf_op jit(solution)/shard_map/all_to_all | solution.py:66
  130.3 1.6 copy-start.8
  130.3 48.6 %collective-permute-start.11 = (bf16[4,3,3,2,16,512]{5,4,3,2,1,0:T(8,128)(2,1)S(1)}, bf16[4,3,3,2,16,512]{5,4,3,2,1,0:T(8,128)(2,1)}, u32[]{:S(2)}, u32[]{:S(2)}) collective-permute-start(bf16[4,3,3,2,16,512]{5,4,3,2,1,0:T(8,128)(2,1)S(1)} %copy-done.1), channel_id=1, source_target_pairs={{0,1},{1,0},{2,3},{3,2},{4,5},{5,4},{6,7},{7,6},{8,9},{9,8},{10,11... | collective-permute-start | bytes 3538952 | tf_op jit(solution)/shard_map/ppermute | solution.py:363
  130.3 28.7 %collective-permute-start.10 = (bf16[4,3,3,2,16,512]{5,4,3,2,1,0:T(8,128)(2,1)}, bf16[4,3,3,2,16,512]{5,4,3,2,1,0:T(8,128)(2,1)}, u32[]{:S(2)}, u32[]{:S(2)}) collective-permute-start(bf16[4,3,3,2,16,512]{5,4,3,2,1,0:T(8,128)(2,1)} %collective-permute-done.8.refs_10_), channel_id=1, source_target_pairs={{0,32},{8,40},{16,48},{24,56},{32,64},{40,72},{48,80},{56,88},{64,... | collective-permute-start | bytes 3538952 | tf_op jit(solution)/shard_map/ppermute | solution.py:360
  131.3 49.5 %collective-permute-start.12 = (bf16[4,3,3,2,16,512]{5,4,3,2,1,0:T(8,128)(2,1)}, bf16[4,3,3,2,16,512]{5,4,3,2,1,0:T(8,128)(2,1)}, u32[]{:S(2)}, u32[]{:S(2)}) collective-permute-start(bf16[4,3,3,2,16,512]{5,4,3,2,1,0:T(8,128)(2,1)} %collective-permute-done.8.refs_10_), channel_id=1, source_target_pairs={{0,1},{1,0},{2,3},{3,2},{4,5},{5,4},{6,7},{7,6},{8,9},{9,8},{10,11... | collective-permute-start | bytes 3538952 | tf_op jit(solution)/shard_map/ppermute | solution.py:363
  131.5 53.0 %collective-permute-start.13 = (bf16[4,3,3,2,16,512]{5,4,3,2,1,0:T(8,128)(2,1)}, bf16[4,3,3,2,16,512]{5,4,3,2,1,0:T(8,128)(2,1)}, u32[]{:S(2)}, u32[]{:S(2)}) collective-permute-start(bf16[4,3,3,2,16,512]{5,4,3,2,1,0:T(8,128)(2,1)} %collective-permute-done.9.refs_11_), channel_id=1, source_target_pairs={{0,1},{1,0},{2,3},{3,2},{4,5},{5,4},{6,7},{7,6},{8,9},{9,8},{10,11... | collective-permute-start | bytes 3538952 | tf_op jit(solution)/shard_map/ppermute | solution.py:363
  159.0 28.9 %collective-permute-start.14 = (bf16[4,3,3,2,16,512]{5,4,3,2,1,0:T(8,128)(2,1)}, bf16[4,3,3,2,16,512]{5,4,3,2,1,0:T(8,128)(2,1)}, u32[]{:S(2)}, u32[]{:S(2)}) collective-permute-start(bf16[4,3,3,2,16,512]{5,4,3,2,1,0:T(8,128)(2,1)} %collective-permute-done.10.refs_12_), channel_id=1, source_target_pairs={{0,1},{1,0},{2,3},{3,2},{4,5},{5,4},{6,7},{7,6},{8,9},{9,8},{10,11... | collective-permute-start | bytes 3538952 | tf_op jit(solution)/shard_map/ppermute | solution.py:363
  175.2 25.9 %collective-permute-start.2 = (bf16[2,4,104,512]{3,2,1,0:T(8,128)(2,1)}, bf16[2,4,104,512]{3,2,1,0:T(8,128)(2,1)S(1)}, u32[]{:S(2)}, u32[]{:S(2)}) collective-permute-start(bf16[2,4,104,512]{3,2,1,0:T(8,128)(2,1)} %get-tuple-element.24.refs_1_), channel_id=1, source_target_pairs={{0,8},{8,16},{16,24},{24,32},{32,40},{40,48},{48,56},{56,64},{64,7... | collective-permute-start | bytes 2555912 | tf_op jit(solution)/shard_map/ppermute | solution.py:32
  178.9 7.2 %collective-permute-start.3 = (bf16[2,1,104,512]{3,2,1,0:T(8,128)(2,1)S(1)}, bf16[2,1,104,512]{3,2,1,0:T(8,128)(2,1)S(1)}, u32[]{:S(2)}, u32[]{:S(2)}) collective-permute-start(bf16[2,1,104,512]{3,2,1,0:T(8,128)(2,1)S(1)} %get-tuple-element.38), channel_id=1, source_target_pairs={{0,1},{1,2},{2,3},{3,4},{4,5},{5,6},{6,7},{8,9},{9,10},{10,11},{11... | collective-permute-start | bytes 638984 | tf_op jit(solution)/shard_map/ppermute | solution.py:32
  180.9 7.0 %collective-permute-start.4 = (bf16[2,1,104,512]{3,2,1,0:T(8,128)(2,1)S(1)}, bf16[2,1,104,512]{3,2,1,0:T(8,128)(2,1)S(1)}, u32[]{:S(2)}, u32[]{:S(2)}) collective-permute-start(bf16[2,1,104,512]{3,2,1,0:T(8,128)(2,1)S(1)} %get-tuple-element.37), channel_id=1, source_target_pairs={{1,0},{2,1},{3,2},{4,3},{5,4},{6,5},{7,6},{9,8},{10,9},{11,10},{12... | collective-permute-start | bytes 638984 | tf_op jit(solution)/shard_map/ppermute | solution.py:32
  186.1 1.8 copy-start.11
  201.1 9.4 %copy-start.7 = (bf16[2,4,104,512]{3,2,1,0:T(8,128)(2,1)}, bf16[2,4,104,512]{3,2,1,0:T(8,128)(2,1)S(1)}, u32[]{:S(2)}) copy-start(bf16[2,4,104,512]{3,2,1,0:T(8,128)(2,1)S(1)} %collective-permute-done.2.refs_1_) | copy-start | bytes 2555908
  201.1 7.6 %collective-permute-start.15 = (bf16[2,1,104,512]{3,2,1,0:T(8,128)(2,1)S(1)}, bf16[2,1,104,512]{3,2,1,0:T(8,128)(2,1)S(1)}, u32[]{:S(2)}, u32[]{:S(2)}) collective-permute-start(bf16[2,1,104,512]{3,2,1,0:T(8,128)(2,1)S(1)} %get-tuple-element.36), channel_id=1, source_target_pairs={{0,1},{1,2},{2,3},{3,4},{4,5},{5,6},{6,7},{8,9},{9,10},{10,11},{11... | collective-permute-start | bytes 638984 | tf_op jit(solution)/shard_map/ppermute | solution.py:32
  204.5 6.0 %collective-permute-start.16 = (bf16[2,1,104,512]{3,2,1,0:T(8,128)(2,1)S(1)}, bf16[2,1,104,512]{3,2,1,0:T(8,128)(2,1)S(1)}, u32[]{:S(2)}, u32[]{:S(2)}) collective-permute-start(bf16[2,1,104,512]{3,2,1,0:T(8,128)(2,1)S(1)} %get-tuple-element.35), channel_id=1, source_target_pairs={{1,0},{2,1},{3,2},{4,3},{5,4},{6,5},{7,6},{9,8},{10,9},{11,10},{12... | collective-permute-start | bytes 638984 | tf_op jit(solution)/shard_map/ppermute | solution.py:32
  208.8 1.8 copy-start.10
  225.1 25.9 %collective-permute-start.17 = (bf16[2,4,104,512]{3,2,1,0:T(8,128)(2,1)}, bf16[2,4,104,512]{3,2,1,0:T(8,128)(2,1)S(1)}, u32[]{:S(2)}, u32[]{:S(2)}) collective-permute-start(bf16[2,4,104,512]{3,2,1,0:T(8,128)(2,1)} %conv_two_behind.1.block_ref), channel_id=1, source_target_pairs={{0,8},{8,16},{16,24},{24,32},{32,40},{40,48},{48,56},{56,64},{64,7... | collective-permute-start | bytes 2555912 | tf_op jit(solution)/shard_map/ppermute | solution.py:32
  (5 other events, 3.7 us)
Sparse Core Ops, SparseCore 0:
  9.0 88.1 all-gather.2
  99.0 36.1 all-gather.4

commit v3 on v2

--- a/solution.py
+++ b/solution.py
@@ -106,9 +106,31 @@
     return lax.optimization_barrier((value, earlier))[0]
 
 
-def quarter_of(weight, low, high, pos):
-    taps = jnp.swapaxes(weight, 3, 4)
-    return lax.dynamic_slice(taps, (0, 0, low, 16 * pos, 0), (3, 3, high - low, 16, CH))
+def quarter_kernel(one_ref, two_ref, place_ref, out_one, out_two, sems):
+    copies = []
+    for k in range(9):
+        rows = pl.multiple_of(place_ref[3] * 16, 16)
+        copies.append(pltpu.make_async_copy(one_ref.at[k % 3, :, k // 3, pl.ds(rows, 16)], out_one.at[k], sems.at[k]))
+    for k in range(3):
+        rows = pl.multiple_of(place_ref[1] * 16, 16)
+        source = two_ref.at[k, :, 2, pl.ds(rows, 16)]
+        copies.append(pltpu.make_async_copy(source, out_two.at[k], sems.at[9 + k]))
+    for copy in copies:
+        copy.start()
+    for copy in copies:
+        copy.wait()
+
+
+def quarters_of(one, two, place):
+    return pl.pallas_call(
+        quarter_kernel,
+        in_specs=[ANY, ANY, SMEM],
+        out_specs=[VMEM] * 2,
+        out_shape=[jax.ShapeDtypeStruct((n, 3, 16, CH), BF16) for n in (9, 3)],
+        scratch_shapes=[pltpu.SemaphoreType.DMA((12,))],
+        cost_estimate=pl.CostEstimate(flops=0, bytes_accessed=10**6, transcendentals=0),
+        name="take_quarters",
+    )(one, two, place)
 
 
 def stack_kernel(*refs):
@@ -124,27 +146,49 @@
     return pl.pallas_call(
         stack_kernel,
         in_specs=[ANY] * len(parts),
-        out_specs=ANY,
-        out_shape=jax.ShapeDtypeStruct((len(parts), *parts[0].shape), parts[0].dtype),
+        out_specs=VMEM,
+        out_shape=jax.ShapeDtypeStruct((len(parts), *parts[0].shape), BF16),
         scratch_shapes=[pltpu.SemaphoreType.DMA((len(parts),))],
+        compiler_params=pltpu.CompilerParams(vmem_limit_bytes=LIMIT),
         cost_estimate=pl.CostEstimate(flops=0, bytes_accessed=4 * 10**6, transcendentals=0),
         name="stack_parts",
     )(*parts)
 
 
-def gather_columns(weight, low, high):
-    return lax.all_gather(jnp.swapaxes(weight[:, :, low:high], 3, 4), "height", axis=3, tiled=True)
+def plane_groups():
+    return [[(4 * y + x) * 8 + 2 * z + c for z in range(4) for x in range(4) for c in range(2)] for y in range(4)]
+
+
+def plane_plan(array):
+    return [
+        (array, (8 * z + 2 * x + c, 3 * e), 0, 3, e, ("fixed", 2 * z + c, None, x))
+        for e in range(3)
+        for z in range(4)
+        for x in range(4)
+        for c in range(2)
+    ]
 
 
 def whole_plan(array, low, high):
-    return [(array, None, e - low, e, ("whole", 0, 0)) for e in range(low, high)]
-
-
-Z_SHIFTS = (0, 3, 1, 2)
-
-
-def ring_plan(array, low, high, flip, step):
-    return [(array, k, e - low, e, (flip, z, step)) for e in range(low, high) for k, z in enumerate(Z_SHIFTS)]
+    return [(array, e - low, 0, 3, e, ("whole", 0, None, 0)) for e in range(low, high)]
+
+
+def shard_plan(array, kind):
+    return [(array, e, 0, 3, e, (kind, 0, None, 0)) for e in (2,)]
+
+
+Z_SHIFTS = (3, 1, 2)
+
+
+def ring_plan(array, begin, end, kind, ring, step):
+    plan = []
+    k = begin
+    while k < end:
+        stop = min(end, k - k % 3 + 3)
+        for i, z in enumerate(Z_SHIFTS):
+            plan.append((array, (i, k - begin), k % 3, stop - k, k // 3, (kind, z, ring, step)))
+        k = stop
+    return plan
 
 
 def conv_kernel(pieces, products, taps, plan, weights, extras, *refs):
@@ -159,17 +203,30 @@
     stat_ref = refs.pop(0) if "stat" in extras else None
     field, wbuf, acc, sems = refs
     low, high = taps[0], taps[-1] + 1
-    core, ring, z = place_ref[0], place_ref[1], place_ref[2]
-    columns = sorted({copy[3] for copy in plan})
-    for array, index, source_e, e, (kind, shift, step) in plan:
+    core, z = place_ref[0], place_ref[2]
+    columns = sorted({copy[4] for copy in plan})
+    for array, index, tap, length, e, (kind, shift, ring, step) in plan:
         slot = columns.index(e)
+        begin, end = max(tap, low), min(tap + length, high)
+        if begin >= end:
+            continue
+        taps_of = pl.ds(begin - low, end - begin)
         if kind == "whole":
-            source, target = w_refs[array].at[pl.ds(low, high - low), :, source_e], wbuf.at[slot]
+            source, target = w_refs[array].at[pl.ds(begin, end - begin), :, index], wbuf.at[slot, taps_of]
         else:
             block = 2 * lax.rem(z + shift, 4) + (1 - core if kind == "other" else core)
-            rows = pl.multiple_of(block * 64 + lax.rem(ring + step, 4) * 16, 16)
-            source = w_refs[array].at[index, pl.ds(low, high - low), :, source_e]
-            target = wbuf.at[slot, :, :, pl.ds(rows, 16)]
+            rows, width = block * 64, 16
+            if kind == "fixed":
+                rows = 64 * shift + 16 * step
+            elif ring is None:
+                width = 64
+            else:
+                rows = rows + lax.rem(place_ref[ring] + step, 4) * 16
+            if kind != "fixed" and ring is None:
+                source = w_refs[array].at[pl.ds(begin, end - begin), :, index]
+            else:
+                source = w_refs[array].at[index[0], pl.ds(index[1] + begin - tap, end - begin)]
+            target = wbuf.at[slot, taps_of, :, pl.ds(pl.multiple_of(rows, 16), width)]
         pltpu.make_async_copy(source, target, sems.at[slot]).start()
     mean, inverse = combine_stats(stats_ref, CELLS * (CH // GROUPS))
     scale = inverse * gain_ref[...]
@@ -216,7 +273,7 @@
 
 def block_conv(name, raws, pieces, products, stats, flags, place, gain, offset, weight, extras, kind, devices):
     arrays, plan = weight
-    columns = len({copy[3] for copy in plan})
+    columns = len({copy[4] for copy in plan})
     taps = sorted({a for _, _, a in products})
     frames = max(f for _, f, _ in products) + 1
     args = [*raws, stats, flags, place, gain, offset, *arrays]
@@ -291,45 +348,80 @@
     )(halo, block, weight, bias)
 
 
-def place_kernel(tokens_ref, line_ref, column_ref, out_ref):
-    tokens = tokens_ref[...]
-    line = line_ref[...]
-    lines = out_ref.shape[0] * RH
+def deal_kernel(tokens_ref, line_ref, column_ref, tile_ref, tile_down_ref, out_ref):
+    tiles = out_ref.shape[0]
+    count = tokens_ref.shape[1]
+    tile = tile_ref[...]
+    same = tile_down_ref[...] == tile
+    earlier = lax.broadcasted_iota(jnp.int32, (count, count), 0) < lax.broadcasted_iota(jnp.int32, (count, count), 1)
+    rank = jnp.sum((same & earlier).astype(F32), axis=0, keepdims=True)
+    slot = tile * 128 + rank.astype(jnp.int32)
+    onto = lax.broadcasted_iota(jnp.int32, (tiles * 128, count), 0) == slot
+    rest = jnp.zeros((14, count), F32)
+    value = [tokens_ref[...].astype(F32), line_ref[...].astype(F32), column_ref[...].astype(F32), rest]
+    value = jnp.concatenate(value, axis=0).astype(BF16)
+    dealt = lax.dot_general(value, onto.astype(F32).astype(BF16), NT, preferred_element_type=F32).astype(BF16)
+    for g in range(tiles):
+        for k in range(3):
+            near = g + k - 1
+            if 0 <= near < tiles:
+                out_ref[g, k] = dealt[:, near * 128 : near * 128 + 128]
+            else:
+                out_ref[g, k] = jnp.zeros((32, 128), BF16)
+
+
+def place_kernel(dealt_ref, first_ref, out_ref):
+    blocks = [dealt_ref[i, k].astype(F32) for i in range(dealt_ref.shape[0]) for k in range(3)]
+    dealt = jnp.concatenate(blocks, axis=1)
+    value, line, column = dealt[:ZC], dealt[ZC : ZC + 1], dealt[ZC + 1 : ZC + 2]
+    count = dealt.shape[1]
+    first = first_ref[0]
+    field = []
+    for t in range(FT):
+        for i in range(RH + 4):
+            row = first + i
+            wanted = jnp.where((row >= 0) & (row < 32), t * 32 + row, -1).astype(F32)
+            field.append(jnp.where(line == wanted, value, 0.0))
+    onto = lax.broadcasted_iota(jnp.int32, (128, count), 0).astype(F32) == column
+    placed = lax.dot_general(
+        jnp.concatenate(field, axis=0).astype(BF16), onto.astype(F32).astype(BF16), NT, preferred_element_type=F32
+    )
+    out_ref[...] = placed.astype(BF16).reshape(out_ref.shape)
+
+
+def latent_own(tokens, token_pos):
+    tiles = lax.axis_size("height")
+    mine = lax.axis_index("height")
     count = tokens.shape[1]
-    zero = jnp.zeros_like(tokens)
-    column = lax.broadcasted_iota(jnp.int32, (128, count), 0) == column_ref[...]
-    column = column.astype(F32).astype(BF16)
-    for t in range(FT):
-        rows = [jnp.where(line == t * lines + h, tokens, zero) for h in range(lines)]
-        placed = lax.dot_general(jnp.concatenate(rows, axis=0), column, NT, preferred_element_type=F32)
-        placed = placed.astype(BF16).reshape(lines, ZC, 128)
-        for g in range(out_ref.shape[0]):
-            first = RH * g - 2
-            for i in range(RH + 4):
-                if 0 <= first + i < lines:
-                    out_ref[g, t, i] = placed[first + i]
-                else:
-                    out_ref[g, t, i] = jnp.zeros((ZC, 128), BF16)
-
-
-def latent_field(tokens, token_pos):
-    tiles = lax.axis_size("height")
-    slab = lax.axis_index("frame")
-    count = tokens.shape[1]
-    places = lax.dynamic_slice_in_dim(token_pos, lax.axis_index("height") * count, count, 0)
-    line = places // WD - slab * (FT * RH * tiles)
+    places = lax.dynamic_slice_in_dim(token_pos, mine * count, count, 0)
+    line = places // WD - lax.axis_index("frame") * (FT * RH * tiles)
     column = places % WD + 1
-    grids = pl.pallas_call(
+    tile = line % (RH * tiles) // RH
+    params = pltpu.CompilerParams(vmem_limit_bytes=LIMIT)
+    cost = pl.CostEstimate(flops=3 * 10**8, bytes_accessed=10**6, transcendentals=0)
+    across = lambda v: v.reshape(1, count)
+    dealt = pl.pallas_call(
+        deal_kernel,
+        in_specs=[VMEM] * 5,
+        out_specs=VMEM,
+        out_shape=jax.ShapeDtypeStruct((tiles, 3, 32, 128), BF16),
+        compiler_params=params,
+        cost_estimate=cost,
+        name="deal_tokens",
+    )(tokens, across(line), across(column), across(tile), tile.reshape(count, 1))
+    dealt = lax.all_to_all(dealt, "height", 0, 0, tiled=True)
+    return pl.pallas_call(
         place_kernel,
-        in_specs=[VMEM] * 3,
+        in_specs=[VMEM, SMEM],
         out_specs=VMEM,
-        out_shape=jax.ShapeDtypeStruct((tiles, FT, RH + 4, ZC, 128), BF16),
-        compiler_params=pltpu.CompilerParams(vmem_limit_bytes=LIMIT),
-        cost_estimate=pl.CostEstimate(flops=3 * 10**8, bytes_accessed=10**6, transcendentals=0),
+        out_shape=jax.ShapeDtypeStruct((FT, RH + 4, ZC, 128), BF16),
+        compiler_params=params,
+        cost_estimate=cost,
         name="place_tokens",
-    )(tokens, line.reshape(1, count), column.reshape(1, count))
-    grids = lax.all_to_all(grids, "height", 0, 0, tiled=True)
-    own = jnp.sum(grids.astype(F32), axis=0).astype(BF16)
+    )(dealt, (mine * RH - 2).reshape(1).astype(jnp.int32))
+
+
+def latent_slabs(own):
     return along(own, "frame", 2), along(own, "frame", 1), own
 
 
@@ -351,8 +443,7 @@
 ):
     devices = lax.axis_size("frame") * lax.axis_size("height")
     slab, tile = lax.axis_index("frame"), lax.axis_index("height")
-    in_y = slab // 4
-    place = jnp.stack([tile % 2, in_y, tile // 2]).astype(jnp.int32)
+    place = jnp.stack([tile % 2, slab // 4, tile // 2, slab % 4]).astype(jnp.int32)
     flags = jnp.stack([slab > 0, tile > 0, tile < lax.axis_size("height") - 1]).astype(F32)
     row = lambda v: v.reshape(1, -1)
 
@@ -365,70 +456,60 @@
     def send_z(v, k):
         return lax.ppermute(v, "height", [(i, (i + 2 * k) % 8) for i in range(8)])
 
-    quarter = quarter_of(weight_two, 1, 3, in_y)
-    sent = [quarter, *[send_z(quarter, k) for k in (1, 3, 2)]]
-    one = gather_columns(weight_one, 0, 3)
-    latent = latent_field(tokens, token_pos)
-    two = gather_columns(after(weight_two, latent[2]), 0, 1)
-    near = stack([after(v, latent[2]) for v in sent])
-    left, right = send_y(near, 1), send_y(near, -1)
-    base, stat = input_conv(latent, weight_in.reshape(-1, CH), row(bias_in), devices)
+    shard_one, shard_two = jnp.swapaxes(weight_one, 3, 4), jnp.swapaxes(weight_two, 3, 4)
+    quarter_one, quarter_two = quarters_of(shard_one, shard_two, place)
+    one = lax.all_gather(quarter_one, ("frame", "height"), axis_index_groups=plane_groups())
+    sent = [send_z(quarter_two, k) for k in (1, 3, 2)]
+    own = latent_own(after(tokens, quarter_one), token_pos)
+    latent = latent_slabs(own)
+    near = stack([after(v, latent[0]) for v in sent])
+    held = [send_y(near, k) if k else near for k in (0, 1, -1, 2)]
+    base, stat = input_conv([after(v, near) for v in latent], weight_in.reshape(-1, CH), row(bias_in), devices)
     shared = share_stats(stat)
-    far = send_y(after(left, shared), 1)
-    swapped = [swap_core(after(v, shared)) for v in (near, left, right)]
+    two = lax.all_gather(after(shard_two, base)[:, :, :2], "height", axis=3, tiled=True)
+    swapped = [swap_core(v) for v in held]
 
     def edges(j):
         return [1] if j == 0 else [2] if j == RH + 1 else []
 
     everything = lambda i, j: ([0] if i < FT else []) + edges(j)
     norm_one = (shared, flags, place, row(gain_one), row(offset_one))
-    common = ([base], [(0, 2 * FT, 0, RH + 2, everything)], [(t, t + a, a) for t in range(FT) for a in range(3)])
+    common = ([after(base, tuple(held))], [(0, 2 * FT, 0, RH + 2, everything)], [(t, t + a, a) for t in range(FT) for a in range(3)])
     inner, stat = block_conv(
         "conv_one",
         *common,
         *norm_one,
-        ([one], whole_plan(0, 0, 3)),
+        ([one], plane_plan(0)),
         {"bias": row(bias_one), "stat": None},
         BF16,
         devices,
     )
     shared = share_stats(stat)
-    behind = along(after(inner, shared), "frame", 1)
-    swapped.append(swap_core(after(far, inner)))
-    arrays = [two, near, left, right, far, *swapped]
-    plan = whole_plan(0, 0, 1)
+    behind = along(inner, "frame", 1)
+    plan = whole_plan(0, 0, 2) + shard_plan(1, "own") + shard_plan(2, "other")
     for k, step in enumerate((0, 3, 1, 2)):
-        plan += ring_plan(1 + k, 1, 3, "own", step) + ring_plan(5 + k, 1, 3, "other", step)
-    kernel_two = (arrays, plan)
+        plan += ring_plan(3 + k, 6, 9, "own", 1, step) + ring_plan(7 + k, 6, 9, "other", 1, step)
+    kernel_two = ([two, shard_two, swap_core(after(shard_two, base)), *held, *swapped], plan)
     norm_two = (shared, flags, place, row(gain_two), row(offset_two))
 
     def rows_around(v):
         return [along(v[:, RH - 1 :], "height", 1), v, along(v[:, :1], "height", -1)]
 
-    pieces = lambda more: [
-        (0, FT, 0, 1, lambda i, j: more + [1]),
-        (0, FT, 1, RH, lambda i, j: more),
-        (0, FT, RH + 1, 1, lambda i, j: more + [2]),
-    ]
-    (partial,) = block_conv(
-        "conv_two_own",
-        rows_around(inner),
-        pieces([]),
-        [(0, 0, 2), (1, 0, 1), (1, 1, 2)],
+    def pieces(frame, more):
+        return [
+            (frame, FT, 0, 1, lambda i, j: more + [1]),
+            (frame, FT, 1, RH, lambda i, j: more),
+            (frame, FT, RH + 1, 1, lambda i, j: more + [2]),
+        ]
+
+    (block,) = block_conv(
+        "conv_two",
+        rows_around(after(behind, shared)) + rows_around(inner),
+        pieces(0, [0]) + pieces(FT, []),
+        [(t, t + a, a) for t in range(FT) for a in range(3)],
         *norm_two,
         kernel_two,
-        {},
-        F32,
-        devices,
-    )
-    (block,) = block_conv(
-        "conv_two_behind",
-        rows_around(after(behind, partial)),
-        pieces([0]),
-        [(0, 0, 0), (0, 1, 1), (1, 1, 0)],
-        *norm_two,
-        kernel_two,
-        {"partial": partial, "bias": row(bias_two), "base": base},
+        {"bias": row(bias_two), "base": base},
         BF16,
         devices,
     )

time: 269 us -> 210 us (0.78)
  Pallas kernels: 99.1 us -> 63.2 us
  blocking collectives: 30.6 us -> 0 us
  starting transfers between devices: 39.6 us -> 53 us
  waiting for transfers between devices: 75.6 us -> 66.5 us
  local copies, waits for them, and re-layouts: 6.85 us -> 10.4 us
    all_to_all x2 -> x0, blocking collectives: 30.6 us -> none  [the longest x1 16.2 us: share_stats(): return lax.all_to_all(stat, ('frame', 'height'), 0, 0, tiled=True)]
    pallas_call x2 -> x4, Pallas kernels: 39.1 us -> 9.36 us  [the longest x1 2.7 us: latent_own(): pl.pallas_call(deal_kernel, in_specs=[VMEM] * 5, out_specs=VMEM, out_shap...]
    ppermute x3, waiting for transfers between devices: 26 us -> 0.01 us  [send_z(): return lax.ppermute(v, 'height', [(i, (i + 2 * k) % 8) for i in range(8)])]
    all_to_all x1 -> x2, starting transfers between devices: 6.45 us -> 16 us  [share_stats(): return lax.all_to_all(stat, ('frame', 'height'), 0, 0, tiled=True)]
    all_gather x2, waiting for transfers between devices: 0.02 us -> 9.31 us  [the longest x1 9.29 us: on_device(): lax.all_gather(quarter_one, ('frame', 'height'), axis_index_groups=plane_...]
    ppermute x8, waiting for transfers between devices: 34.4 us -> 42.3 us  [along(): lax.ppermute(value, axis, [(source, source + steps) for source in range(l...]
    pallas_call x3 -> x2, Pallas kernels: 46.1 us -> 39.9 us  [block_conv(): pl.pallas_call(functools.partial(conv_kernel, pieces, products, taps, pla...]
    all_to_all x1 -> x2, waiting for transfers between devices: 7 us -> 1.43 us  [share_stats(): return lax.all_to_all(stat, ('frame', 'height'), 0, 0, tiled=True)]
  transfers between devices with their start and end apart: 21 -> 24, of which waited for: 11 -> 12; matrix products, arithmetic and copies ran while one was open for 2% -> 4% of each run, Pallas kernels for 29% -> 15%
where the time goes in v3:
time: 210 us; the launch traced here: 209 us
  waiting for transfers between devices  66.5 us (32%)
  Pallas kernels  63.2 us (30%)
  starting transfers between devices  53 us (25%)
  between operations  13.7 us (7%)
  local copies, waits for them, and re-layouts  10.4 us (5%)
    ppermute x8, waiting for transfers between devices, along(): lax.ppermute(value, axis, [(source, source + steps) for source in range(l...  42.3 us
    pallas_call x2, Pallas kernels, block_conv(): pl.pallas_call(functools.partial(conv_kernel, pieces, products, taps, pla...  39.9 us
    ppermute x8, starting transfers between devices, along(): lax.ppermute(value, axis, [(source, source + steps) for source in range(l...  21.9 us
    all_to_all x2, starting transfers between devices, share_stats(): return lax.all_to_all(stat, ('frame', 'height'), 0, 0, tiled=True)  16 us
    ppermute x3, waiting for transfers between devices, send_y(): lax.ppermute(v, 'frame', [(4 * y + x, 4 * ((y + k) % 4) + x) for y in ran...  10.1 us
    all_gather x1, waiting for transfers between devices, on_device(): lax.all_gather(quarter_one, ('frame', 'height'), axis_index_groups=plane_...  9.29 us
    pallas_call x1, Pallas kernels, upsample(): pl.pallas_call(upsample_kernel, grid=(FT, 2), in_specs=[pl.BlockSpec((FT,...  8.93 us
    all_to_all x1, starting transfers between devices, latent_own(): dealt = lax.all_to_all(dealt, 'height', 0, 0, tiled=True)  5.41 us
  transfers between devices with their start and end apart: 24, of which 12 were waited for; matrix products, arithmetic and copies ran while one was open for 4% of the time, Pallas kernels for 15%

profile of v3, /device:TPU:40, one launch (start us, length us, event | category | flops | bytes accessed | tf_op | source)
XLA Modules:
  0.0 208.8 jit_solution(281664064071488599)
XLA Ops:
  7.1 2.7 %take_quarters.1 = (bf16[9,3,16,512]{3,2,1,0:T(8,128)(2,1)}, bf16[3,3,16,512]{3,2,1,0:T(8,128)(2,1)}) custom-call(bf16[3,3,3,64,512]{4,3,2,1,0:T(8,128)(2,1)} %bitcast.32, bf16[3,3,3,64,512]{4,3,2,1,0:T(8,128)(2,1)} %bitcast.28, s32[4]{0:T(128)} %pad_add_fusion.place_ref.refs_3_.refs_8_), custom_call_target="tpu_custom_call" | custom-call | bytes 1000000 | tf_op jit(solution)/shard_map/take_quarters/pallas_call | solution.py:125
  13.4 2.7 %deal_tokens.1 = bf16[8,3,32,128]{3,2,1,0:T(8,128)(2,1)} custom-call(bf16[16,832]{1,0:T(8,128)(2,1)} %tokens_ref, s32[1,832]{1,0:T(1,128)} %reshape.46.line_ref, s32[1,832]{1,0:T(1,128)} %reshape.47.column_ref, s32[1,832]{1,0:T(1,128)} %reshape.48.tile_ref, s32[832,1]{1,0:T(8,128)} %reshape.61.tile_down_ref), custom_call_target="tpu_custom_call" | custom-call | flops 300000000 | bytes 1000000 | tf_op jit(solution)/shard_map/deal_tokens/pallas_call | solution.py:403
  16.1 5.4 %all-to-all-start = ((bf16[8,3,32,128]{3,2,1,0:T(8,128)(2,1)}), bf16[8,3,32,128]{3,2,1,0:T(8,128)(2,1)S(1)}, u32[]{:S(2)}, u32[]{:S(2)}) async-start(bf16[8,3,32,128]{3,2,1,0:T(8,128)(2,1)} %deal_tokens.1), calls=%async_computation | async-start | bytes 393216 | tf_op jit(solution)/shard_map/all_to_all | solution.py:412
  21.5 2.1 collective-permute-start.3
  23.5 1.5 collective-permute-start.2
  25.6 3.4 %all-to-all-done.dealt_ref = bf16[8,3,32,128]{3,2,1,0:T(8,128)(2,1)S(1)} async-done(((bf16[8,3,32,128]{3,2,1,0:T(8,128)(2,1)}), bf16[8,3,32,128]{3,2,1,0:T(8,128)(2,1)S(1)}, u32[]{:S(2)}, u32[]{:S(2)}) %all-to-all-start) | async-done | bytes 196640 | tf_op jit(solution)/shard_map/all_to_all | solution.py:412
  29.6 2.1 %place_tokens.1.own_ref = bf16[2,8,16,128]{3,2,1,0:T(8,128)(2,1)} custom-call(bf16[8,3,32,128]{3,2,1,0:T(8,128)(2,1)} %copy-done.4, s32[1]{0:T(128)} %bitcast.6.first_ref), custom_call_target="tpu_custom_call" | custom-call | flops 300000000 | bytes 1000000 | tf_op jit(solution)/shard_map/place_tokens/pallas_call | solution.py:413
  31.7 5.0 %collective-permute-start = (bf16[2,8,16,128]{3,2,1,0:T(8,128)(2,1)}, bf16[2,8,16,128]{3,2,1,0:T(8,128)(2,1)S(1)}, u32[]{:S(2)}, u32[]{:S(2)}) collective-permute-start(bf16[2,8,16,128]{3,2,1,0:T(8,128)(2,1)} %place_tokens.1.own_ref), channel_id=1, source_target_pairs={{0,16},{8,24},{16,32},{24,40},{32,48},{40,56},{48,64},{56,72},{64,... | collective-permute-start | bytes 196616 | tf_op jit(solution)/shard_map/ppermute | solution.py:32
  36.7 2.5 %collective-permute-start.4 = (bf16[2,8,16,128]{3,2,1,0:T(8,128)(2,1)}, bf16[2,8,16,128]{3,2,1,0:T(8,128)(2,1)S(1)}, u32[]{:S(2)}, u32[]{:S(2)}) collective-permute-start(bf16[2,8,16,128]{3,2,1,0:T(8,128)(2,1)} %place_tokens.1.own_ref), channel_id=1, source_target_pairs={{0,8},{8,16},{16,24},{24,32},{32,40},{40,48},{48,56},{56,64},{64,7... | collective-permute-start | bytes 196616 | tf_op jit(solution)/shard_map/ppermute | solution.py:32
  39.3 2.1 collective-permute-done.early_ref
  42.7 1.8 stack_parts.1.refs_14_
  45.8 5.0 %input_conv.1 = (bf16[4,6,104,512]{3,2,1,0:T(8,128)(2,1)}, f32[128,128]{1,0:T(8,128)}) custom-call(bf16[2,8,16,128]{3,2,1,0:T(8,128)(2,1)} %copy-done.13, bf16[2,8,16,128]{3,2,1,0:T(8,128)(2,1)} %copy-done.14, bf16[2,8,16,128]{3,2,1,0:T(8,128)(2,1)} %place_tokens.1.own_ref, bf16[432,512]{1,0:T(8,128)(2,1)} %bitcast.38, f32[1,512]{1,0:T(1,128)} %bitcast.39), custom_call_target="tpu_custom_call" | custom-call | flops 3000000000 | bytes 4000000 | tf_op jit(solution)/shard_map/input_conv/pallas_call | solution.py:91
  52.1 1.7 collective-permute-start.5
  54.1 2.7 %collective-permute-start.7 = (bf16[3,3,3,16,512]{4,3,2,1,0:T(8,128)(2,1)S(1)}, bf16[3,3,3,16,512]{4,3,2,1,0:T(8,128)(2,1)S(1)}, u32[]{:S(2)}, u32[]{:S(2)}) collective-permute-start(bf16[3,3,3,16,512]{4,3,2,1,0:T(8,128)(2,1)S(1)} %copy-done.2), channel_id=1, source_target_pairs={{0,64},{8,72},{16,80},{24,88},{32,96},{40,104},{48,112},{56,120},{... | collective-permute-start | bytes 1327112 | tf_op jit(solution)/shard_map/ppermute | solution.py:451
  56.9 6.0 %all-to-all-start.1 = ((f32[128,1,128]{2,1,0:T(1,128)}), f32[128,1,128]{2,1,0:T(1,128)S(1)}, u32[]{:S(2)}, u32[]{:S(2)}) async-start(f32[128,1,128]{2,1,0:T(1,128)} %bitcast.10), calls=%async_computation.1 | async-start | bytes 131072 | tf_op jit(solution)/shard_map/all_to_all | solution.py:66
  63.7 7.2 %collective-permute-done.5.refs_15_ = bf16[3,3,3,16,512]{4,3,2,1,0:T(8,128)(2,1)} collective-permute-done((bf16[3,3,3,16,512]{4,3,2,1,0:T(8,128)(2,1)S(1)}, bf16[3,3,3,16,512]{4,3,2,1,0:T(8,128)(2,1)}, u32[]{:S(2)}, u32[]{:S(2)}) %collective-permute-start.5) | collective-permute-done | bytes 442400 | tf_op jit(solution)/shard_map/ppermute | solution.py:451
  70.9 2.9 %collective-permute-done.7.refs_17_ = bf16[3,3,3,16,512]{4,3,2,1,0:T(8,128)(2,1)S(1)} collective-permute-done((bf16[3,3,3,16,512]{4,3,2,1,0:T(8,128)(2,1)S(1)}, bf16[3,3,3,16,512]{4,3,2,1,0:T(8,128)(2,1)S(1)}, u32[]{:S(2)}, u32[]{:S(2)}) %collective-permute-start.7) | collective-permute-done | bytes 442400 | tf_op jit(solution)/shard_map/ppermute | solution.py:451
  75.1 9.3 %all-gather.6.cloned.1.call-done = bf16[288,3,16,512]{3,2,1,0:T(8,128)(2,1)} async-done(((bf16[9,3,16,512]{3,2,1,0:T(8,128)(2,1)}), bf16[288,3,16,512]{3,2,1,0:T(8,128)(2,1)}) %all-gather.6.cloned.1.call-update) | async-done | bytes 14155792 | tf_op jit(solution)/shard_map/all_gather | solution.py:461
  84.3 20.1 %conv_one.1 = (bf16[2,4,104,512]{3,2,1,0:T(8,128)(2,1)}, f32[128,128]{1,0:T(8,128)}) custom-call(bf16[4,6,104,512]{3,2,1,0:T(8,128)(2,1)} %get-tuple-element.31.refs_0_.refs_23_, f32[128,128]{1,0:T(8,128)} %bitcast.35, f32[3]{0:T(128)} %add_convert_fusion.refs_2_.refs_7_, s32[4]{0:T(128)} %pad_add_fusion.place_ref.refs_3_.refs_8_, f32[1,512]{1,0:T(1,128)} %bitcast.40, ...), custom_call_target="tpu_custom_call" | custom-call | flops 12683575296 | bytes 16000000 | tf_op jit(solution)/shard_map/conv_one/pallas_call | solution.py:286
  104.5 2.4 %collective-permute-start.8 = (bf16[2,4,104,512]{3,2,1,0:T(8,128)(2,1)}, bf16[2,4,104,512]{3,2,1,0:T(8,128)(2,1)S(1)}, u32[]{:S(2)}, u32[]{:S(2)}) collective-permute-start(bf16[2,4,104,512]{3,2,1,0:T(8,128)(2,1)} %get-tuple-element.33.refs_4_), channel_id=1, source_target_pairs={{0,8},{8,16},{16,24},{24,32},{32,40},{40,48},{48,56},{56,64},{64,7... | collective-permute-start | bytes 2555912 | tf_op jit(solution)/shard_map/ppermute | solution.py:32
  107.6 10.0 %all-to-all-start.2 = ((f32[128,1,128]{2,1,0:T(1,128)}), f32[128,1,128]{2,1,0:T(1,128)S(1)}, u32[]{:S(2)}, u32[]{:S(2)}) async-start(f32[128,1,128]{2,1,0:T(1,128)} %bitcast.34), calls=%async_computation.2 | async-start | bytes 131072 | tf_op jit(solution)/shard_map/all_to_all | solution.py:66
  117.5 13.0 %collective-permute-done.8.refs_1_ = bf16[2,4,104,512]{3,2,1,0:T(8,128)(2,1)S(1)} collective-permute-done((bf16[2,4,104,512]{3,2,1,0:T(8,128)(2,1)}, bf16[2,4,104,512]{3,2,1,0:T(8,128)(2,1)S(1)}, u32[]{:S(2)}, u32[]{:S(2)}) %collective-permute-start.8) | collective-permute-done | bytes 852000 | tf_op jit(solution)/shard_map/ppermute | solution.py:32
  130.6 2.1 %fusion.7 = (bf16[2,1,104,512]{3,2,1,0:T(8,128)(2,1)S(1)}, bf16[2,1,104,512]{3,2,1,0:T(8,128)(2,1)}) fusion(bf16[2,4,104,512]{3,2,1,0:T(8,128)(2,1)} %get-tuple-element.33.refs_4_), kind=kLoop, calls=%fused_computation.20 | loop fusion | bytes 851968 | tf_op jit(solution)/shard_map/slice | solution.py:496
  133.6 1.9 collective-permute-start.11
  135.5 3.6 %collective-permute-start.12 = (bf16[2,1,104,512]{3,2,1,0:T(8,128)(2,1)S(1)}, bf16[2,1,104,512]{3,2,1,0:T(8,128)(2,1)S(1)}, u32[]{:S(2)}, u32[]{:S(2)}) collective-permute-start(bf16[2,1,104,512]{3,2,1,0:T(8,128)(2,1)S(1)} %get-tuple-element.39), channel_id=1, source_target_pairs={{1,0},{2,1},{3,2},{4,3},{5,4},{6,5},{7,6},{9,8},{10,9},{11,10},{12... | collective-permute-start | bytes 638984 | tf_op jit(solution)/shard_map/ppermute | solution.py:32
  139.2 1.9 collective-permute-start.10
  141.1 2.6 %collective-permute-start.9 = (bf16[2,1,104,512]{3,2,1,0:T(8,128)(2,1)S(1)}, bf16[2,1,104,512]{3,2,1,0:T(8,128)(2,1)}, u32[]{:S(2)}, u32[]{:S(2)}) collective-permute-start(bf16[2,1,104,512]{3,2,1,0:T(8,128)(2,1)S(1)} %get-tuple-element.42), channel_id=1, source_target_pairs={{0,1},{1,2},{2,3},{3,4},{4,5},{5,6},{6,7},{8,9},{9,10},{10,11},{11... | collective-permute-start | bytes 638984 | tf_op jit(solution)/shard_map/ppermute | solution.py:32
  144.9 3.5 %collective-permute-done.9.refs_0_ = bf16[2,1,104,512]{3,2,1,0:T(8,128)(2,1)} collective-permute-done((bf16[2,1,104,512]{3,2,1,0:T(8,128)(2,1)S(1)}, bf16[2,1,104,512]{3,2,1,0:T(8,128)(2,1)}, u32[]{:S(2)}, u32[]{:S(2)}) %collective-permute-start.9) | collective-permute-done | bytes 213024 | tf_op jit(solution)/shard_map/ppermute | solution.py:32
  148.4 19.8 %conv_two.1.block_ref = bf16[2,4,104,512]{3,2,1,0:T(8,128)(2,1)} custom-call(bf16[2,1,104,512]{3,2,1,0:T(8,128)(2,1)} %collective-permute-done.9.refs_0_, bf16[2,4,104,512]{3,2,1,0:T(8,128)(2,1)} %copy-done.3, bf16[2,1,104,512]{3,2,1,0:T(8,128)(2,1)} %collective-permute-done.10.refs_2_, bf16[2,1,104,512]{3,2,1,0:T(8,128)(2,1)} %copy-done.11, ...), custom_call_target="tpu_custom_call" | custom-call | flops 12683575296 | bytes 16000000 | tf_op jit(solution)/shard_map/conv_two/pallas_call | solution.py:286
  168.2 1.9 collective-permute-start.18
  170.1 22.0 %collective-permute-done.18.halo_ref = bf16[2,4,104,512]{3,2,1,0:T(8,128)(2,1)S(1)} collective-permute-done((bf16[2,4,104,512]{3,2,1,0:T(8,128)(2,1)}, bf16[2,4,104,512]{3,2,1,0:T(8,128)(2,1)S(1)}, u32[]{:S(2)}, u32[]{:S(2)}) %collective-permute-start.18) | collective-permute-done | bytes 852000 | tf_op jit(solution)/shard_map/ppermute | solution.py:32
  193.1 8.9 %upsample.1 = bf16[4,8,208,512]{3,2,1,0:T(8,128)(2,1)} custom-call(bf16[2,4,104,512]{3,2,1,0:T(8,128)(2,1)} %copy-done.1, bf16[2,4,104,512]{3,2,1,0:T(8,128)(2,1)} %conv_two.1.block_ref, bf16[3,512,1024]{2,1,0:T(8,128)(2,1)} %w_ref.1, f32[1,1024]{1,0:T(1,128)} %bitcast.36), custom_call_target="tpu_custom_call" | custom-call | flops 3000000000 | bytes 12000000 | tf_op jit(solution)/shard_map/upsample/pallas_call | solution.py:334
  (66 shorter events, 15.2 us)
Async XLA Ops:
  6.5 77.8 %all-gather.6.cloned.1.call-start = ((), (), s32[]{:S(2)}) async-start(), calls=%async_computation.4 | async-start | bytes 14598144 | tf_op jit(solution)/shard_map/all_gather | solution.py:461
  16.1 12.9 %all-to-all-start = ((bf16[8,3,32,128]{3,2,1,0:T(8,128)(2,1)}), bf16[8,3,32,128]{3,2,1,0:T(8,128)(2,1)S(1)}, u32[]{:S(2)}, u32[]{:S(2)}) async-start(bf16[8,3,32,128]{3,2,1,0:T(8,128)(2,1)} %deal_tokens.1), calls=%async_computation | async-start | bytes 393216 | tf_op jit(solution)/shard_map/all_to_all | solution.py:412
  21.5 122.3 %all-gather.4.cloned.1.call-start = ((), (), s32[]{:S(2)}) async-start(), calls=%async_computation.3 | async-start | bytes 10616832 | tf_op jit(solution)/shard_map/all_gather | solution.py:469
  21.5 17.8 %collective-permute-start.3 = (bf16[3,3,16,512]{3,2,1,0:T(8,128)(2,1)}, bf16[3,3,16,512]{3,2,1,0:T(8,128)(2,1)S(1)}, u32[]{:S(2)}, u32[]{:S(2)}) collective-permute-start(bf16[3,3,16,512]{3,2,1,0:T(8,128)(2,1)} %get-tuple-element.23), channel_id=1, source_target_pairs={{0,4},{1,5},{2,6},{3,7},{4,0},{5,1},{6,2},{7,3},{8,12},{9,13},{10,... | collective-permute-start | bytes 442376 | tf_op jit(solution)/shard_map/ppermute | solution.py:457
  23.5 17.8 %collective-permute-start.2 = (bf16[3,3,16,512]{3,2,1,0:T(8,128)(2,1)}, bf16[3,3,16,512]{3,2,1,0:T(8,128)(2,1)S(1)}, u32[]{:S(2)}, u32[]{:S(2)}) collective-permute-start(bf16[3,3,16,512]{3,2,1,0:T(8,128)(2,1)} %get-tuple-element.23), channel_id=1, source_target_pairs={{0,6},{1,7},{2,0},{3,1},{4,2},{5,3},{6,4},{7,5},{8,14},{9,15},{10,... | collective-permute-start | bytes 442376 | tf_op jit(solution)/shard_map/ppermute | solution.py:457
  25.0 16.4 %collective-permute-start.1 = (bf16[3,3,16,512]{3,2,1,0:T(8,128)(2,1)}, bf16[3,3,16,512]{3,2,1,0:T(8,128)(2,1)S(1)}, u32[]{:S(2)}, u32[]{:S(2)}) collective-permute-start(bf16[3,3,16,512]{3,2,1,0:T(8,128)(2,1)} %get-tuple-element.23), channel_id=1, source_target_pairs={{0,2},{1,3},{2,4},{3,5},{4,6},{5,7},{6,0},{7,1},{8,10},{9,11},{10,... | collective-permute-start | bytes 442376 | tf_op jit(solution)/shard_map/ppermute | solution.py:457
  31.7 9.6 %collective-permute-start = (bf16[2,8,16,128]{3,2,1,0:T(8,128)(2,1)}, bf16[2,8,16,128]{3,2,1,0:T(8,128)(2,1)S(1)}, u32[]{:S(2)}, u32[]{:S(2)}) collective-permute-start(bf16[2,8,16,128]{3,2,1,0:T(8,128)(2,1)} %place_tokens.1.own_ref), channel_id=1, source_target_pairs={{0,16},{8,24},{16,32},{24,40},{32,48},{40,56},{48,64},{56,72},{64,... | collective-permute-start | bytes 196616 | tf_op jit(solution)/shard_map/ppermute | solution.py:32
  36.7 8.5 %collective-permute-start.4 = (bf16[2,8,16,128]{3,2,1,0:T(8,128)(2,1)}, bf16[2,8,16,128]{3,2,1,0:T(8,128)(2,1)S(1)}, u32[]{:S(2)}, u32[]{:S(2)}) collective-permute-start(bf16[2,8,16,128]{3,2,1,0:T(8,128)(2,1)} %place_tokens.1.own_ref), channel_id=1, source_target_pairs={{0,8},{8,16},{16,24},{24,32},{32,40},{40,48},{48,56},{56,64},{64,7... | collective-permute-start | bytes 196616 | tf_op jit(solution)/shard_map/ppermute | solution.py:32
  41.4 3.9 %copy-start.13 = (bf16[2,8,16,128]{3,2,1,0:T(8,128)(2,1)}, bf16[2,8,16,128]{3,2,1,0:T(8,128)(2,1)S(1)}, u32[]{:S(2)}) copy-start(bf16[2,8,16,128]{3,2,1,0:T(8,128)(2,1)S(1)} %collective-permute-done.early_ref) | copy-start | bytes 196612
  45.8 5.0 %copy-start = (bf16[3,3,3,512,64]{3,4,2,1,0:T(8,128)(2,1)S(1)}, bf16[3,3,3,512,64]{3,4,2,1,0:T(8,128)(2,1)}, u32[]{:S(2)}) copy-start(bf16[3,3,3,512,64]{3,4,2,1,0:T(8,128)(2,1)} %param.24) | copy-start | bytes 5308420
  52.1 18.8 %collective-permute-start.5 = (bf16[3,3,3,16,512]{4,3,2,1,0:T(8,128)(2,1)S(1)}, bf16[3,3,3,16,512]{4,3,2,1,0:T(8,128)(2,1)}, u32[]{:S(2)}, u32[]{:S(2)}) collective-permute-start(bf16[3,3,3,16,512]{4,3,2,1,0:T(8,128)(2,1)S(1)} %copy-done.2), channel_id=1, source_target_pairs={{0,32},{8,40},{16,48},{24,56},{32,64},{40,72},{48,80},{56,88},{64,... | collective-permute-start | bytes 1327112 | tf_op jit(solution)/shard_map/ppermute | solution.py:451
  53.8 17.0 %collective-permute-start.6 = (bf16[3,3,3,16,512]{4,3,2,1,0:T(8,128)(2,1)S(1)}, bf16[3,3,3,16,512]{4,3,2,1,0:T(8,128)(2,1)}, u32[]{:S(2)}, u32[]{:S(2)}) collective-permute-start(bf16[3,3,3,16,512]{4,3,2,1,0:T(8,128)(2,1)S(1)} %copy-done.2), channel_id=1, source_target_pairs={{0,96},{8,104},{16,112},{24,120},{32,0},{40,8},{48,16},{56,24},{64... | collective-permute-start | bytes 1327112 | tf_op jit(solution)/shard_map/ppermute | solution.py:451
  54.1 19.7 %collective-permute-start.7 = (bf16[3,3,3,16,512]{4,3,2,1,0:T(8,128)(2,1)S(1)}, bf16[3,3,3,16,512]{4,3,2,1,0:T(8,128)(2,1)S(1)}, u32[]{:S(2)}, u32[]{:S(2)}) collective-permute-start(bf16[3,3,3,16,512]{4,3,2,1,0:T(8,128)(2,1)S(1)} %copy-done.2), channel_id=1, source_target_pairs={{0,64},{8,72},{16,80},{24,88},{32,96},{40,104},{48,112},{56,120},{... | collective-permute-start | bytes 1327112 | tf_op jit(solution)/shard_map/ppermute | solution.py:451
  56.9 18.2 %all-to-all-start.1 = ((f32[128,1,128]{2,1,0:T(1,128)}), f32[128,1,128]{2,1,0:T(1,128)S(1)}, u32[]{:S(2)}, u32[]{:S(2)}) async-start(f32[128,1,128]{2,1,0:T(1,128)} %bitcast.10), calls=%async_computation.1 | async-start | bytes 131072 | tf_op jit(solution)/shard_map/all_to_all | solution.py:66
  63.6 80.2 %collective-permute-start.13 = (bf16[3,3,3,64,512]{4,3,2,1,0:T(8,128)(2,1)S(1)}, bf16[3,3,3,64,512]{4,3,2,1,0:T(8,128)(2,1)}, u32[]{:S(2)}, u32[]{:S(2)}) collective-permute-start(bf16[3,3,3,64,512]{4,3,2,1,0:T(8,128)(2,1)S(1)} %bitcast.31), channel_id=1, source_target_pairs={{0,1},{1,0},{2,3},{3,2},{4,5},{5,4},{6,7},{7,6},{8,9},{9,8},{10,11... | collective-permute-start | bytes 5308424 | tf_op jit(solution)/shard_map/ppermute | solution.py:454
  73.8 30.6 %copy-start.10 = (bf16[3,3,3,16,512]{4,3,2,1,0:T(8,128)(2,1)}, bf16[3,3,3,16,512]{4,3,2,1,0:T(8,128)(2,1)S(1)}, u32[]{:S(2)}) copy-start(bf16[3,3,3,16,512]{4,3,2,1,0:T(8,128)(2,1)S(1)} %collective-permute-done.7.refs_17_) | copy-start | bytes 1327108
  75.1 9.3 %copy-start.9 = (f32[128,1,128]{2,1,0:T(1,128)}, f32[128,1,128]{2,1,0:T(1,128)S(1)}, u32[]{:S(2)}) copy-start(f32[128,1,128]{2,1,0:T(1,128)S(1)} %all-to-all-done.1) | copy-start | bytes 196612
  104.5 26.1 %collective-permute-start.8 = (bf16[2,4,104,512]{3,2,1,0:T(8,128)(2,1)}, bf16[2,4,104,512]{3,2,1,0:T(8,128)(2,1)S(1)}, u32[]{:S(2)}, u32[]{:S(2)}) collective-permute-start(bf16[2,4,104,512]{3,2,1,0:T(8,128)(2,1)} %get-tuple-element.33.refs_4_), channel_id=1, source_target_pairs={{0,8},{8,16},{16,24},{24,32},{32,40},{40,48},{48,56},{56,64},{64,7... | collective-permute-start | bytes 2555912 | tf_op jit(solution)/shard_map/ppermute | solution.py:32
  106.9 26.7 %collective-permute-start.14 = (bf16[3,3,3,16,512]{4,3,2,1,0:T(8,128)(2,1)S(1)}, bf16[3,3,3,16,512]{4,3,2,1,0:T(8,128)(2,1)}, u32[]{:S(2)}, u32[]{:S(2)}) collective-permute-start(bf16[3,3,3,16,512]{4,3,2,1,0:T(8,128)(2,1)S(1)} %copy-done.2), channel_id=1, source_target_pairs={{0,1},{1,0},{2,3},{3,2},{4,5},{5,4},{6,7},{7,6},{8,9},{9,8},{10,11... | collective-permute-start | bytes 1327112 | tf_op jit(solution)/shard_map/ppermute | solution.py:454
  107.0 28.5 %collective-permute-start.15 = (bf16[3,3,3,16,512]{4,3,2,1,0:T(8,128)(2,1)}, bf16[3,3,3,16,512]{4,3,2,1,0:T(8,128)(2,1)}, u32[]{:S(2)}, u32[]{:S(2)}) collective-permute-start(bf16[3,3,3,16,512]{4,3,2,1,0:T(8,128)(2,1)} %collective-permute-done.5.refs_15_), channel_id=1, source_target_pairs={{0,1},{1,0},{2,3},{3,2},{4,5},{5,4},{6,7},{7,6},{8,9},{9,8},{10,11... | collective-permute-start | bytes 1327112 | tf_op jit(solution)/shard_map/ppermute | solution.py:454
  107.5 31.7 %collective-permute-start.16 = (bf16[3,3,3,16,512]{4,3,2,1,0:T(8,128)(2,1)}, bf16[3,3,3,16,512]{4,3,2,1,0:T(8,128)(2,1)}, u32[]{:S(2)}, u32[]{:S(2)}) collective-permute-start(bf16[3,3,3,16,512]{4,3,2,1,0:T(8,128)(2,1)} %collective-permute-done.6.refs_16_), channel_id=1, source_target_pairs={{0,1},{1,0},{2,3},{3,2},{4,5},{5,4},{6,7},{7,6},{8,9},{9,8},{10,11... | collective-permute-start | bytes 1327112 | tf_op jit(solution)/shard_map/ppermute | solution.py:454
  107.6 25.3 %all-to-all-start.2 = ((f32[128,1,128]{2,1,0:T(1,128)}), f32[128,1,128]{2,1,0:T(1,128)S(1)}, u32[]{:S(2)}, u32[]{:S(2)}) async-start(f32[128,1,128]{2,1,0:T(1,128)} %bitcast.34), calls=%async_computation.2 | async-start | bytes 131072 | tf_op jit(solution)/shard_map/all_to_all | solution.py:66
  130.6 17.8 %copy-start.3 = (bf16[2,4,104,512]{3,2,1,0:T(8,128)(2,1)}, bf16[2,4,104,512]{3,2,1,0:T(8,128)(2,1)S(1)}, u32[]{:S(2)}) copy-start(bf16[2,4,104,512]{3,2,1,0:T(8,128)(2,1)S(1)} %collective-permute-done.8.refs_1_) | copy-start | bytes 2555908
  130.6 10.5 %collective-permute-start.17 = (bf16[3,3,3,16,512]{4,3,2,1,0:T(8,128)(2,1)}, bf16[3,3,3,16,512]{4,3,2,1,0:T(8,128)(2,1)}, u32[]{:S(2)}, u32[]{:S(2)}) collective-permute-start(bf16[3,3,3,16,512]{4,3,2,1,0:T(8,128)(2,1)} %copy-done.10), channel_id=1, source_target_pairs={{0,1},{1,0},{2,3},{3,2},{4,5},{5,4},{6,7},{7,6},{8,9},{9,8},{10,11... | collective-permute-start | bytes 1327112 | tf_op jit(solution)/shard_map/ppermute | solution.py:454
  132.9 15.5 %copy-start.8 = (f32[128,1,128]{2,1,0:T(1,128)}, f32[128,1,128]{2,1,0:T(1,128)S(1)}, u32[]{:S(2)}) copy-start(f32[128,1,128]{2,1,0:T(1,128)S(1)} %all-to-all-done.2) | copy-start | bytes 196612
  133.6 10.2 %collective-permute-start.11 = (bf16[2,1,104,512]{3,2,1,0:T(8,128)(2,1)}, bf16[2,1,104,512]{3,2,1,0:T(8,128)(2,1)S(1)}, u32[]{:S(2)}, u32[]{:S(2)}) collective-permute-start(bf16[2,1,104,512]{3,2,1,0:T(8,128)(2,1)} %get-tuple-element.40), channel_id=1, source_target_pairs={{0,1},{1,2},{2,3},{3,4},{4,5},{5,6},{6,7},{8,9},{9,10},{10,11},{11... | collective-permute-start | bytes 638984 | tf_op jit(solution)/shard_map/ppermute | solution.py:32
  135.5 8.3 %collective-permute-start.12 = (bf16[2,1,104,512]{3,2,1,0:T(8,128)(2,1)S(1)}, bf16[2,1,104,512]{3,2,1,0:T(8,128)(2,1)S(1)}, u32[]{:S(2)}, u32[]{:S(2)}) collective-permute-start(bf16[2,1,104,512]{3,2,1,0:T(8,128)(2,1)S(1)} %get-tuple-element.39), channel_id=1, source_target_pairs={{1,0},{2,1},{3,2},{4,3},{5,4},{6,5},{7,6},{9,8},{10,9},{11,10},{12... | collective-permute-start | bytes 638984 | tf_op jit(solution)/shard_map/ppermute | solution.py:32
  139.2 5.7 %collective-permute-start.10 = (bf16[2,1,104,512]{3,2,1,0:T(8,128)(2,1)}, bf16[2,1,104,512]{3,2,1,0:T(8,128)(2,1)}, u32[]{:S(2)}, u32[]{:S(2)}) collective-permute-start(bf16[2,1,104,512]{3,2,1,0:T(8,128)(2,1)} %get-tuple-element.41), channel_id=1, source_target_pairs={{1,0},{2,1},{3,2},{4,3},{5,4},{6,5},{7,6},{9,8},{10,9},{11,10},{12... | collective-permute-start | bytes 638984 | tf_op jit(solution)/shard_map/ppermute | solution.py:32
  141.1 7.3 %collective-permute-start.9 = (bf16[2,1,104,512]{3,2,1,0:T(8,128)(2,1)S(1)}, bf16[2,1,104,512]{3,2,1,0:T(8,128)(2,1)}, u32[]{:S(2)}, u32[]{:S(2)}) collective-permute-start(bf16[2,1,104,512]{3,2,1,0:T(8,128)(2,1)S(1)} %get-tuple-element.42), channel_id=1, source_target_pairs={{0,1},{1,2},{2,3},{3,4},{4,5},{5,6},{6,7},{8,9},{9,10},{10,11},{11... | collective-permute-start | bytes 638984 | tf_op jit(solution)/shard_map/ppermute | solution.py:32
  143.8 4.6 %copy-start.11 = (bf16[2,1,104,512]{3,2,1,0:T(8,128)(2,1)}, bf16[2,1,104,512]{3,2,1,0:T(8,128)(2,1)S(1)}, u32[]{:S(2)}) copy-start(bf16[2,1,104,512]{3,2,1,0:T(8,128)(2,1)S(1)} %collective-permute-done.11.refs_3_) | copy-start | bytes 638980
  143.8 4.6 %copy-start.12 = (bf16[2,1,104,512]{3,2,1,0:T(8,128)(2,1)}, bf16[2,1,104,512]{3,2,1,0:T(8,128)(2,1)S(1)}, u32[]{:S(2)}) copy-start(bf16[2,1,104,512]{3,2,1,0:T(8,128)(2,1)S(1)} %collective-permute-done.12.refs_5_) | copy-start | bytes 638980
  168.2 23.9 %collective-permute-start.18 = (bf16[2,4,104,512]{3,2,1,0:T(8,128)(2,1)}, bf16[2,4,104,512]{3,2,1,0:T(8,128)(2,1)S(1)}, u32[]{:S(2)}, u32[]{:S(2)}) collective-permute-start(bf16[2,4,104,512]{3,2,1,0:T(8,128)(2,1)} %conv_two.1.block_ref), channel_id=1, source_target_pairs={{0,8},{8,16},{16,24},{24,32},{32,40},{40,48},{48,56},{56,64},{64,7... | collective-permute-start | bytes 2555912 | tf_op jit(solution)/shard_map/ppermute | solution.py:32
  (7 other events, 7.0 us)
Sparse Core Ops, SparseCore 0:
  10.0 74.3 all-gather.5
  86.0 54.1 all-gather.3
